TPU v7x, 512 devices: a whole 4x4x16 slice. The times are simulated.
512 devices in a mesh: seq: 128 (over x, y, z_hi, core), ch: 4 (over z_lo).
Axes of the slice: x: 4, y: 4, z: 16 (z_hi: 4, z_lo: 4; z = z_hi * 4 + z_lo), core: 2. Of those that a mesh axis runs over, the one named last changes fastest.
Arguments:
- signal_branch: bfloat16 [64, 65536], P('ch', 'seq'), may hold values from -6 to 6
- leading_multiplier: bfloat16 [64, 65536], P('ch', 'seq'), may hold values from -6 to 6
- trailing_multiplier: bfloat16 [64, 65536], P('ch', 'seq'), may hold values from -6 to 6
- loss_upstream_adjoint: bfloat16 [64, 65536], P('ch', 'seq'), may hold values from -6 to 6
- kernel_net_hidden: bfloat16 [64, 65536], P('ch', 'seq'), may hold values from -6 to 6
- kernel_readout_matrix: float32 [2, 64, 64], P(None, 'ch'), may hold values from -0.75 to 0.75
- kernel_attenuation: float32 [2, 64], P(None, 'ch'), may hold values from 7.6293945e-06 to 0.033333335
Outputs:
- signal_branch_adjoint: bfloat16 [64, 65536], P('ch', 'seq')
- leading_multiplier_adjoint: bfloat16 [64, 65536], P('ch', 'seq')
- trailing_multiplier_adjoint: bfloat16 [64, 65536], P('ch', 'seq')
- readout_adjoint_factored: bfloat16 [2, 64, 64], P(None, 'ch')
- hidden_adjoint_factored: bfloat16 [64, 65536], P('ch', 'seq')
All inputs are finite; a program needn't handle non-finite values.
Results may differ from a plain program's by a relative error of at most 0.003.
Values may be sent and summed in bfloat16 or wider, within the bound.
A program may use at most 64 MiB of HBM per device.

v0:
```python
import math

import jax
import jax.numpy as jnp
from jax import lax
from jax.sharding import PartitionSpec as P


def trig_pair(counts, modulus):
    angle = -2.0 * math.pi * counts.astype(jnp.float32) / modulus
    return (jnp.cos(angle), jnp.sin(angle))


def make_tables(seq_count, locus_entries, seq_index):
    total = 2 * seq_count * locus_entries
    slabs = locus_entries // seq_count
    blocks = locus_entries // 128
    sources = jnp.arange(seq_count, dtype=jnp.int32)
    coarse = jnp.arange(2, dtype=jnp.int32)[:, None] * seq_count + sources[None, :]
    cross = sources[:, None, None] * coarse[None, :, :] % (2 * seq_count)
    cross_cos, cross_sin = trig_pair(cross, 2 * seq_count)
    local = jnp.arange(slabs, dtype=jnp.int32)[:, None] * seq_count + seq_index
    twist = local[None, :, :] * coarse[:, None, :] % total
    twist_cos, twist_sin = trig_pair(twist, total)
    block_ids = jnp.arange(blocks, dtype=jnp.int32)
    lanes = jnp.arange(128, dtype=jnp.int32)
    outer_cos, outer_sin = trig_pair(block_ids[:, None] * block_ids[None, :] % blocks, blocks)
    inner_tw = block_ids[:, None] * lanes[None, :] % locus_entries
    inner_cos, inner_sin = trig_pair(inner_tw, locus_entries)
    lane_cos, lane_sin = trig_pair(lanes[:, None] * lanes[None, :] % 128, 128)
    return (
        cross_cos,
        cross_sin,
        twist_cos,
        twist_sin,
        outer_cos,
        outer_sin,
        inner_cos,
        inner_sin,
        lane_cos,
        lane_sin,
        total,
    )


def to_spectrum(columns, tables):
    highest = lax.Precision.HIGHEST
    (
        cross_cos,
        cross_sin,
        twist_cos,
        twist_sin,
        outer_cos,
        outer_sin,
        inner_cos,
        inner_sin,
        lane_cos,
        lane_sin,
        total,
    ) = tables
    real_y = jnp.einsum("xrq,qjd->xjrd", columns, cross_cos, precision=highest)
    imag_y = jnp.einsum("xrq,qjd->xjrd", columns, cross_sin, precision=highest)
    real_z = real_y * twist_cos - imag_y * twist_sin
    imag_z = real_y * twist_sin + imag_y * twist_cos
    real_z, imag_z = (
        lax.all_to_all(real_z, "seq", split_axis=3, concat_axis=3, tiled=True),
        lax.all_to_all(imag_z, "seq", split_axis=3, concat_axis=3, tiled=True),
    )
    real_a = jnp.einsum("xjab,ak->xjkb", real_z, outer_cos, precision=highest) - jnp.einsum(
        "xjab,ak->xjkb", imag_z, outer_sin, precision=highest
    )
    imag_a = jnp.einsum("xjab,ak->xjkb", real_z, outer_sin, precision=highest) + jnp.einsum(
        "xjab,ak->xjkb", imag_z, outer_cos, precision=highest
    )
    real_t = real_a * inner_cos - imag_a * inner_sin
    imag_t = real_a * inner_sin + imag_a * inner_cos
    real_s = jnp.einsum("xjkb,bl->xjkl", real_t, lane_cos, precision=highest) - jnp.einsum(
        "xjkb,bl->xjkl", imag_t, lane_sin, precision=highest
    )
    imag_s = jnp.einsum("xjkb,bl->xjkl", real_t, lane_sin, precision=highest) + jnp.einsum(
        "xjkb,bl->xjkl", imag_t, lane_cos, precision=highest
    )
    return (real_s, imag_s)


def from_spectrum(real_part, imag_part, tables):
    highest = lax.Precision.HIGHEST
    (
        cross_cos,
        cross_sin,
        twist_cos,
        twist_sin,
        outer_cos,
        outer_sin,
        inner_cos,
        inner_sin,
        lane_cos,
        lane_sin,
        total,
    ) = tables
    real_b = jnp.einsum("xjkl,bl->xjkb", real_part, lane_cos, precision=highest) + jnp.einsum(
        "xjkl,bl->xjkb", imag_part, lane_sin, precision=highest
    )
    imag_b = jnp.einsum("xjkl,bl->xjkb", imag_part, lane_cos, precision=highest) - jnp.einsum(
        "xjkl,bl->xjkb", real_part, lane_sin, precision=highest
    )
    real_t = real_b * inner_cos + imag_b * inner_sin
    imag_t = imag_b * inner_cos - real_b * inner_sin
    real_a = jnp.einsum("xjkb,ak->xjab", real_t, outer_cos, precision=highest) + jnp.einsum(
        "xjkb,ak->xjab", imag_t, outer_sin, precision=highest
    )
    imag_a = jnp.einsum("xjkb,ak->xjab", imag_t, outer_cos, precision=highest) - jnp.einsum(
        "xjkb,ak->xjab", real_t, outer_sin, precision=highest
    )
    real_a, imag_a = (
        lax.all_to_all(real_a, "seq", split_axis=3, concat_axis=3, tiled=True),
        lax.all_to_all(imag_a, "seq", split_axis=3, concat_axis=3, tiled=True),
    )
    real_p = real_a * twist_cos + imag_a * twist_sin
    imag_p = imag_a * twist_cos - real_a * twist_sin
    summed = jnp.einsum("xjrd,qjd->xrq", real_p, cross_cos, precision=highest) + jnp.einsum(
        "xjrd,qjd->xrq", imag_p, cross_sin, precision=highest
    )
    return summed / total


def inverse_real(spec, tables):
    return from_spectrum(spec[0], spec[1], tables)


def complex_mul(left, right):
    return (left[0] * right[0] - left[1] * right[1], left[0] * right[1] + left[1] * right[0])


def conjugate(spec):
    return (spec[0], -spec[1])


def take_slot(spec, slot, width):
    return (spec[0][slot * width : (slot + 1) * width], spec[1][slot * width : (slot + 1) * width])


def join_specs(specs):
    return (
        jnp.concatenate([item[0] for item in specs], 0),
        jnp.concatenate([item[1] for item in specs], 0),
    )


def body(
    signal_branch,
    leading_multiplier,
    trailing_multiplier,
    loss_upstream_adjoint,
    kernel_net_hidden,
    kernel_readout_matrix,
    kernel_attenuation,
):
    highest = lax.Precision.HIGHEST
    seq_count = lax.axis_size("seq")
    seq_index = lax.axis_index("seq")
    embedding_width, locus_entries = signal_branch.shape
    genome_extent = seq_count * locus_entries
    slabs = locus_entries // seq_count
    tables = make_tables(seq_count, locus_entries, seq_index)
    position = (seq_index * locus_entries + jnp.arange(locus_entries, dtype=jnp.int32)).astype(
        jnp.float32
    )
    window = jnp.exp(-kernel_attenuation[:, :, None] * position)
    scale = jnp.sqrt(
        jnp.expm1(-2.0 * kernel_attenuation) / jnp.expm1(-2.0 * kernel_attenuation * genome_extent)
    )
    feat_full = lax.all_gather(kernel_net_hidden, "ch", axis=0, tiled=True).astype(jnp.float32)
    base = jnp.einsum("ocf,fl->ocl", kernel_readout_matrix, feat_full, precision=highest)
    filt = base * window * scale[:, :, None]

    def spectra(stack):
        moved = lax.all_to_all(
            stack.reshape(stack.shape[0], slabs, seq_count),
            "seq",
            split_axis=2,
            concat_axis=2,
            tiled=True,
        )
        return to_spectrum(moved, tables)

    def signals(spec):
        columns = inverse_real(spec, tables)
        moved = lax.all_to_all(columns, "seq", split_axis=2, concat_axis=2, tiled=True)
        return moved.reshape(columns.shape[0], locus_entries)

    branch_source = signal_branch.astype(jnp.float32)
    gate_a = leading_multiplier.astype(jnp.float32)
    gate_b = trailing_multiplier.astype(jnp.float32)
    grad_y = loss_upstream_adjoint.astype(jnp.float32)
    filt_one = filt[0]
    filt_two = filt[1]
    grad_two = grad_y * gate_b
    first = spectra(jnp.concatenate([branch_source, filt_one, filt_two], 0))
    spec_v = take_slot(first, 0, embedding_width)
    spec_h1 = take_slot(first, 1, embedding_width)
    spec_h2 = take_slot(first, 2, embedding_width)
    first_u = signals(complex_mul(spec_v, spec_h1))
    second_z = gate_a * first_u
    second = spectra(jnp.concatenate([second_z, grad_two], 0))
    spec_z = take_slot(second, 0, embedding_width)
    spec_g2 = take_slot(second, 1, embedding_width)
    back_two = signals(
        join_specs(
            [
                complex_mul(spec_z, spec_h2),
                complex_mul(spec_g2, conjugate(spec_h2)),
                complex_mul(spec_g2, conjugate(spec_z)),
            ]
        )
    )
    second_u = back_two[:embedding_width]
    grad_z = back_two[embedding_width : 2 * embedding_width]
    grad_h2 = back_two[2 * embedding_width :]
    grad_one = grad_z * gate_a
    spec_g1 = spectra(grad_one)
    back_three = signals(
        join_specs(
            [complex_mul(spec_g1, conjugate(spec_h1)), complex_mul(spec_g1, conjugate(spec_v))]
        )
    )
    branch_adjoint = back_three[:embedding_width]
    grad_h1 = back_three[embedding_width:]
    collected_pieces = jnp.concatenate(
        [branch_adjoint, grad_z * first_u, grad_y * second_u, grad_h1, grad_h2], 0
    )
    signal_branch_adjoint = collected_pieces[:embedding_width].astype(jnp.bfloat16)
    leading_multiplier_adjoint = collected_pieces[embedding_width : 2 * embedding_width].astype(
        jnp.bfloat16
    )
    trailing_multiplier_adjoint = collected_pieces[
        2 * embedding_width : 3 * embedding_width
    ].astype(jnp.bfloat16)
    filter_grads = collected_pieces[3 * embedding_width :].reshape(
        2, embedding_width, locus_entries
    )
    dhw = filter_grads * window * scale[:, :, None] / math.sqrt(genome_extent)
    partial_w = jnp.einsum("ocl,fl->ocf", dhw, feat_full, precision=highest)
    readout_adjoint_factored = lax.psum(partial_w, "seq").astype(jnp.bfloat16)
    flat_weight = kernel_readout_matrix.reshape(2 * embedding_width, kernel_readout_matrix.shape[2])
    flat_dhw = dhw.reshape(2 * embedding_width, locus_entries)
    hidden_adjoint_factored = lax.psum_scatter(
        jnp.einsum("ef,el->fl", flat_weight, flat_dhw, precision=highest),
        "ch",
        scatter_dimension=0,
        tiled=True,
    ).astype(jnp.bfloat16)
    return (
        signal_branch_adjoint,
        leading_multiplier_adjoint,
        trailing_multiplier_adjoint,
        readout_adjoint_factored,
        hidden_adjoint_factored,
    )


def solution(mesh):
    in_specs = (
        P("ch", "seq"),
        P("ch", "seq"),
        P("ch", "seq"),
        P("ch", "seq"),
        P("ch", "seq"),
        P(None, "ch", None),
        P(None, "ch"),
    )
    out_specs = (
        P("ch", "seq"),
        P("ch", "seq"),
        P("ch", "seq"),
        P(None, "ch", None),
        P("ch", "seq"),
    )
    return jax.shard_map(body, mesh=mesh, in_specs=in_specs, out_specs=out_specs, check_vma=False)
```

profile of v0, /device:TPU:1, one launch (start us, length us, event | category | flops | bytes accessed | tf_op | source)
XLA Modules:
  0.0 1366.4 jit_solution(18410245248936466922)
XLA Ops:
  8.7 12.2 all_gather.3
  22.2 24.0 %all-to-all-start = ((f32[128,1,192]{2,1,0:T(1,128)}), f32[128,1,192]{2,1,0:T(1,128)S(1)}, u32[]{:S(2)}, u32[]{:S(2)}) async-start(f32[128,1,192]{2,1,0:T(1,128)} %reshape.185), calls=%async_computation | async-start | bytes 262144 | tf_op jit(solution)/shard_map/all_to_all | solution.py:178
  46.4 18.2 %all-to-all-done = f32[128,1,192]{2,1,0:T(1,128)S(1)} async-done(((f32[128,1,192]{2,1,0:T(1,128)}), f32[128,1,192]{2,1,0:T(1,128)S(1)}, u32[]{:S(2)}, u32[]{:S(2)}) %all-to-all-start) | async-done | bytes 98336 | tf_op jit(solution)/shard_map/all_to_all | solution.py:178
  78.0 17.5 %all-to-all-done.1 = f32[128,1,384]{2,1,0:T(1,128)S(1)} async-done(((f32[128,1,384]{2,1,0:T(1,128)}), f32[128,1,384]{2,1,0:T(1,128)S(1)}, u32[]{:S(2)}, u32[]{:S(2)}) %all-to-all-start.1) | async-done | bytes 196640 | tf_op jit(solution)/shard_map/all_to_all | solution.py:66
  108.2 15.8 %all-to-all-done.2 = f32[128,1,384]{2,1,0:T(1,128)S(1)} async-done(((f32[128,1,384]{2,1,0:T(1,128)}), f32[128,1,384]{2,1,0:T(1,128)S(1)}, u32[]{:S(2)}, u32[]{:S(2)}) %all-to-all-start.2) | async-done | bytes 196640 | tf_op jit(solution)/shard_map/all_to_all | solution.py:67
  133.4 10.7 all-to-all-start.4
  146.0 15.2 %all-to-all-done.4 = f32[128,1,128]{2,1,0:T(1,128)S(1)} async-done(((f32[128,1,128]{2,1,0:T(1,128)}), f32[128,1,128]{2,1,0:T(1,128)S(1)}, u32[]{:S(2)}, u32[]{:S(2)}) %all-to-all-start.4) | async-done | bytes 65568 | tf_op jit(solution)/shard_map/all_to_all | solution.py:117
  168.8 16.0 %all-to-all-done.3 = f32[128,1,128]{2,1,0:T(1,128)S(1)} async-done(((f32[128,1,128]{2,1,0:T(1,128)}), f32[128,1,128]{2,1,0:T(1,128)S(1)}, u32[]{:S(2)}, u32[]{:S(2)}) %all-to-all-start.3) | async-done | bytes 65568 | tf_op jit(solution)/shard_map/all_to_all | solution.py:116
  194.9 20.6 %all-to-all-done.5 = f32[16,4,128]{0,1,2:T(4,128)S(1)} async-done(((f32[16,4,128]{0,1,2:T(4,128)}), f32[16,4,128]{0,1,2:T(4,128)S(1)}, u32[]{:S(2)}, u32[]{:S(2)}) %all-to-all-start.5) | async-done | bytes 32800 | tf_op jit(solution)/shard_map/all_to_all | solution.py:189
  216.0 27.4 %all_to_all.90 = f32[128,1,128]{2,1,0:T(1,128)S(1)} all-to-all(f32[128,1,128]{2,1,0:T(1,128)S(1)} %reshape.195), channel_id=1, replica_groups=mesh['seq'=128,'ch'=4] {'seq'}, dimensions={0} | all-to-all | bytes 131072 | tf_op jit(solution)/shard_map/all_to_all | solution.py:178
  254.7 16.7 %all-to-all-done.7 = f32[128,1,256]{2,1,0:T(1,128)S(1)} async-done(((f32[128,1,256]{2,1,0:T(1,128)}), f32[128,1,256]{2,1,0:T(1,128)S(1)}, u32[]{:S(2)}, u32[]{:S(2)}) %all-to-all-start.7) | async-done | bytes 131104 | tf_op jit(solution)/shard_map/all_to_all | solution.py:66
  280.8 15.1 %all-to-all-done.8 = f32[128,1,256]{2,1,0:T(1,128)S(1)} async-done(((f32[128,1,256]{2,1,0:T(1,128)}), f32[128,1,256]{2,1,0:T(1,128)S(1)}, u32[]{:S(2)}, u32[]{:S(2)}) %all-to-all-start.8) | async-done | bytes 131104 | tf_op jit(solution)/shard_map/all_to_all | solution.py:67
  316.9 15.9 %all-to-all-done.9 = f32[128,1,384]{2,1,0:T(1,128)S(1)} async-done(((f32[128,1,384]{2,1,0:T(1,128)}), f32[128,1,384]{2,1,0:T(1,128)S(1)}, u32[]{:S(2)}, u32[]{:S(2)}) %all-to-all-start.9) | async-done | bytes 196640 | tf_op jit(solution)/shard_map/all_to_all | solution.py:116
  332.7 10.1 all-to-all-start.10
  344.7 16.4 %all-to-all-done.10 = f32[128,1,384]{2,1,0:T(1,128)S(1)} async-done(((f32[128,1,384]{2,1,0:T(1,128)}), f32[128,1,384]{2,1,0:T(1,128)S(1)}, u32[]{:S(2)}, u32[]{:S(2)}) %all-to-all-start.10) | async-done | bytes 196640 | tf_op jit(solution)/shard_map/all_to_all | solution.py:117
  365.0 28.0 %all_to_all.91 = f32[128,1,192]{2,1,0:T(1,128)S(1)} all-to-all(f32[128,1,192]{2,1,0:T(1,128)S(1)} %reshape.205), channel_id=1, replica_groups=mesh['seq'=128,'ch'=4] {'seq'}, dimensions={0} | all-to-all | bytes 196608 | tf_op jit(solution)/shard_map/all_to_all | solution.py:189
  395.4 26.5 %all_to_all.92 = f32[16,4,128]{0,1,2:T(4,128)S(1)} all-to-all(f32[16,4,128]{0,1,2:T(4,128)S(1)} %copy.295), channel_id=1, replica_groups=mesh['seq'=128,'ch'=4] {'seq'}, dimensions={2} | all-to-all | bytes 65536 | tf_op jit(solution)/shard_map/all_to_all | solution.py:178
  424.8 11.4 all-to-all-start.13
  437.5 15.7 %all-to-all-done.13 = f32[128,1,128]{2,1,0:T(1,128)S(1)} async-done(((f32[128,1,128]{2,1,0:T(1,128)}), f32[128,1,128]{2,1,0:T(1,128)S(1)}, u32[]{:S(2)}, u32[]{:S(2)}) %all-to-all-start.13) | async-done | bytes 65568 | tf_op jit(solution)/shard_map/all_to_all | solution.py:66
  462.4 14.7 %all-to-all-done.14 = f32[128,1,128]{2,1,0:T(1,128)S(1)} async-done(((f32[128,1,128]{2,1,0:T(1,128)}), f32[128,1,128]{2,1,0:T(1,128)S(1)}, u32[]{:S(2)}, u32[]{:S(2)}) %all-to-all-start.14) | async-done | bytes 65568 | tf_op jit(solution)/shard_map/all_to_all | solution.py:67
  494.2 15.8 %all-to-all-done.15 = f32[128,1,256]{2,1,0:T(1,128)S(1)} async-done(((f32[128,1,256]{2,1,0:T(1,128)}), f32[128,1,256]{2,1,0:T(1,128)S(1)}, u32[]{:S(2)}, u32[]{:S(2)}) %all-to-all-start.15) | async-done | bytes 131104 | tf_op jit(solution)/shard_map/all_to_all | solution.py:116
  518.9 17.5 %all-to-all-done.16 = f32[128,1,256]{2,1,0:T(1,128)S(1)} async-done(((f32[128,1,256]{2,1,0:T(1,128)}), f32[128,1,256]{2,1,0:T(1,128)S(1)}, u32[]{:S(2)}, u32[]{:S(2)}) %all-to-all-start.16) | async-done | bytes 131104 | tf_op jit(solution)/shard_map/all_to_all | solution.py:117
  547.2 16.9 %all-to-all-done.17 = f32[128,1,128]{2,1,0:T(1,128)S(1)} async-done(((f32[128,1,128]{2,1,0:T(1,128)}), f32[128,1,128]{2,1,0:T(1,128)S(1)}, u32[]{:S(2)}, u32[]{:S(2)}) %all-to-all-start.17) | async-done | bytes 65568 | tf_op jit(solution)/shard_map/all_to_all | solution.py:189
  568.0 789.6 %psum.7 = bf16[2,16,64]{2,1,0:T(8,128)(2,1)} all-reduce(f32[2,16,64]{2,1,0:T(8,128)S(1)} %fusion.110), channel_id=1, replica_groups=mesh['seq'=128,'ch'=4] {'seq'}, use_global_device_ids=true, to_apply=%region_0.1 | all-reduce | flops 2048 | bytes 12288 | tf_op jit(solution)/shard_map/psum | solution.py:244
  (207 shorter events, 162.8 us)
Async XLA Ops:
  7.2 13.6 copy-start
  7.2 0.7 copy-start.5
  7.9 0.8 copy-start.3
  22.2 42.5 %all-to-all-start = ((f32[128,1,192]{2,1,0:T(1,128)}), f32[128,1,192]{2,1,0:T(1,128)S(1)}, u32[]{:S(2)}, u32[]{:S(2)}) async-start(f32[128,1,192]{2,1,0:T(1,128)} %reshape.185), calls=%async_computation | async-start | bytes 262144 | tf_op jit(solution)/shard_map/all_to_all | solution.py:178
  69.6 25.9 %all-to-all-start.1 = ((f32[128,1,384]{2,1,0:T(1,128)}), f32[128,1,384]{2,1,0:T(1,128)S(1)}, u32[]{:S(2)}, u32[]{:S(2)}) async-start(f32[128,1,384]{2,1,0:T(1,128)} %reshape.187), calls=%async_computation.1 | async-start | bytes 393216 | tf_op jit(solution)/shard_map/all_to_all | solution.py:66
  95.5 28.4 %all-to-all-start.2 = ((f32[128,1,384]{2,1,0:T(1,128)}), f32[128,1,384]{2,1,0:T(1,128)S(1)}, u32[]{:S(2)}, u32[]{:S(2)}) async-start(f32[128,1,384]{2,1,0:T(1,128)} %reshape.189), calls=%async_computation.2 | async-start | bytes 393216 | tf_op jit(solution)/shard_map/all_to_all | solution.py:67
  133.4 27.8 %all-to-all-start.4 = ((f32[128,1,128]{2,1,0:T(1,128)}), f32[128,1,128]{2,1,0:T(1,128)S(1)}, u32[]{:S(2)}, u32[]{:S(2)}) async-start(f32[128,1,128]{2,1,0:T(1,128)} %reshape.191), calls=%async_computation.4 | async-start | bytes 131072 | tf_op jit(solution)/shard_map/all_to_all | solution.py:117
  161.2 23.5 %all-to-all-start.3 = ((f32[128,1,128]{2,1,0:T(1,128)}), f32[128,1,128]{2,1,0:T(1,128)S(1)}, u32[]{:S(2)}, u32[]{:S(2)}) async-start(f32[128,1,128]{2,1,0:T(1,128)} %reshape.193), calls=%async_computation.3 | async-start | bytes 131072 | tf_op jit(solution)/shard_map/all_to_all | solution.py:116
  188.5 6.3 copy-start.2
  188.5 6.3 copy-start.4
  188.5 26.9 %all-to-all-start.5 = ((f32[16,4,128]{0,1,2:T(4,128)}), f32[16,4,128]{0,1,2:T(4,128)S(1)}, u32[]{:S(2)}, u32[]{:S(2)}) async-start(f32[16,4,128]{0,1,2:T(4,128)} %copy.264), calls=%async_computation.5 | async-start | bytes 524288 | tf_op jit(solution)/shard_map/all_to_all | solution.py:189
  194.9 20.7 %copy-start.1 = (bf16[16,512]{1,0:T(8,128)(2,1)S(1)}, bf16[16,512]{1,0:T(8,128)(2,1)}, u32[]{:S(2)}) copy-start(bf16[16,512]{1,0:T(8,128)(2,1)} %param.8) | copy-start | bytes 49156
  247.3 24.1 %all-to-all-start.7 = ((f32[128,1,256]{2,1,0:T(1,128)}), f32[128,1,256]{2,1,0:T(1,128)S(1)}, u32[]{:S(2)}, u32[]{:S(2)}) async-start(f32[128,1,256]{2,1,0:T(1,128)} %reshape.197), calls=%async_computation.7 | async-start | bytes 262144 | tf_op jit(solution)/shard_map/all_to_all | solution.py:66
  271.4 24.5 %all-to-all-start.8 = ((f32[128,1,256]{2,1,0:T(1,128)}), f32[128,1,256]{2,1,0:T(1,128)S(1)}, u32[]{:S(2)}, u32[]{:S(2)}) async-start(f32[128,1,256]{2,1,0:T(1,128)} %reshape.199), calls=%async_computation.8 | async-start | bytes 262144 | tf_op jit(solution)/shard_map/all_to_all | solution.py:67
  305.4 27.3 %all-to-all-start.9 = ((f32[128,1,384]{2,1,0:T(1,128)}), f32[128,1,384]{2,1,0:T(1,128)S(1)}, u32[]{:S(2)}, u32[]{:S(2)}) async-start(f32[128,1,384]{2,1,0:T(1,128)} %reshape.201), calls=%async_computation.9 | async-start | bytes 393216 | tf_op jit(solution)/shard_map/all_to_all | solution.py:116
  332.7 28.3 %all-to-all-start.10 = ((f32[128,1,384]{2,1,0:T(1,128)}), f32[128,1,384]{2,1,0:T(1,128)S(1)}, u32[]{:S(2)}, u32[]{:S(2)}) async-start(f32[128,1,384]{2,1,0:T(1,128)} %reshape.203), calls=%async_computation.10 | async-start | bytes 393216 | tf_op jit(solution)/shard_map/all_to_all | solution.py:117
  424.8 28.5 %all-to-all-start.13 = ((f32[128,1,128]{2,1,0:T(1,128)}), f32[128,1,128]{2,1,0:T(1,128)S(1)}, u32[]{:S(2)}, u32[]{:S(2)}) async-start(f32[128,1,128]{2,1,0:T(1,128)} %reshape.207), calls=%async_computation.13 | async-start | bytes 131072 | tf_op jit(solution)/shard_map/all_to_all | solution.py:66
  453.3 23.9 %all-to-all-start.14 = ((f32[128,1,128]{2,1,0:T(1,128)}), f32[128,1,128]{2,1,0:T(1,128)S(1)}, u32[]{:S(2)}, u32[]{:S(2)}) async-start(f32[128,1,128]{2,1,0:T(1,128)} %reshape.209), calls=%async_computation.14 | async-start | bytes 131072 | tf_op jit(solution)/shard_map/all_to_all | solution.py:67
  485.4 24.6 %all-to-all-start.15 = ((f32[128,1,256]{2,1,0:T(1,128)}), f32[128,1,256]{2,1,0:T(1,128)S(1)}, u32[]{:S(2)}, u32[]{:S(2)}) async-start(f32[128,1,256]{2,1,0:T(1,128)} %reshape.211), calls=%async_computation.15 | async-start | bytes 262144 | tf_op jit(solution)/shard_map/all_to_all | solution.py:116
  510.0 26.4 %all-to-all-start.16 = ((f32[128,1,256]{2,1,0:T(1,128)}), f32[128,1,256]{2,1,0:T(1,128)S(1)}, u32[]{:S(2)}, u32[]{:S(2)}) async-start(f32[128,1,256]{2,1,0:T(1,128)} %reshape.213), calls=%async_computation.16 | async-start | bytes 262144 | tf_op jit(solution)/shard_map/all_to_all | solution.py:117
  540.4 23.7 %all-to-all-start.17 = ((f32[128,1,128]{2,1,0:T(1,128)}), f32[128,1,128]{2,1,0:T(1,128)S(1)}, u32[]{:S(2)}, u32[]{:S(2)}) async-start(f32[128,1,128]{2,1,0:T(1,128)} %reshape.215), calls=%async_computation.17 | async-start | bytes 131072 | tf_op jit(solution)/shard_map/all_to_all | solution.py:189
  546.9 810.8 %reduce-scatter.2.cloned.1.call-start = ((), (), s32[]{:S(2)}) async-start(), calls=%async_computation.19 | async-start | bytes 163840 | tf_op jit(solution)/shard_map/reduce_scatter | solution.py:247
Sparse Core Ops, SparseCore 0:
  566.5 16.9 reduce-scatter.1
where the time goes:
time: 1380 us; the launch traced here: 1370 us
  blocking collectives  884 us (64%)
  waiting for transfers between devices  248 us (18%)
  starting transfers between devices  134 us (10%)
  matrix products  34.2 us (2%)
  local copies, waits for them, and re-layouts  32.3 us (2%)
  other arithmetic  18.1 us (1%)
  between operations  15.6 us (1%)
    psum x1, blocking collectives, body(): readout_adjoint_factored = lax.psum(partial_w, 'seq').astype(jnp.bfloat16)  790 us
    all_to_all x2, blocking collectives, spectra(): lax.all_to_all(stack.reshape(stack.shape[0], slabs, seq_count), 'seq', sp...  53.9 us
    all_to_all x3, waiting for transfers between devices, to_spectrum(): lax.all_to_all(real_z, 'seq', split_axis=3, concat_axis=3, tiled=True)  49.9 us
    all_to_all x3, waiting for transfers between devices, from_spectrum(): lax.all_to_all(imag_a, 'seq', split_axis=3, concat_axis=3, tiled=True)  49.1 us
    all_to_all x3, waiting for transfers between devices, from_spectrum(): lax.all_to_all(real_a, 'seq', split_axis=3, concat_axis=3, tiled=True)  47.7 us
    all_to_all x3, waiting for transfers between devices, to_spectrum(): lax.all_to_all(imag_z, 'seq', split_axis=3, concat_axis=3, tiled=True)  45.6 us
    all_to_all x2, waiting for transfers between devices, signals(): lax.all_to_all(columns, 'seq', split_axis=2, concat_axis=2, tiled=True)  37.5 us
    all_to_all x3, starting transfers between devices, from_spectrum(): lax.all_to_all(imag_a, 'seq', split_axis=3, concat_axis=3, tiled=True)  28.2 us
  transfers between devices with their start and end apart: 16, of which 15 were waited for; matrix products, arithmetic and copies ran while one was open for 2% of the time, Pallas kernels for 0%

commit v1 on v0

v1 whole, which is shorter than its diff:
```python
import math

import jax
import jax.numpy as jnp
import ml_dtypes
import numpy as np
from jax import lax
from jax.experimental import pallas as pl
from jax.experimental.pallas import tpu as pltpu
from jax.sharding import PartitionSpec as P

F32 = jnp.float32
BF16 = jnp.bfloat16
SEQ = 128
CH = 4
WIDTH = 16
LOCUS = 512
MESH = pl.DeviceIdType.MESH


def owner_of(channel, group):
    high = lax.rem(lax.div(channel, 4) + lax.rem(channel, 4) + group, 4)
    return channel * 8 + 2 * high


def halves(value):
    high = value.astype(BF16)
    return high, (value - high.astype(F32)).astype(BF16)


def np_halves(value):
    value = value.astype(np.float32)
    high = value.astype(ml_dtypes.bfloat16)
    return high, (value - high.astype(np.float32)).astype(ml_dtypes.bfloat16)


def make_tables():
    length = SEQ * LOCUS
    points = 2 * length
    order = np.concatenate([2 * np.arange(128), 2 * np.arange(128) + 1])
    coarse = np.arange(256) + 0.5
    angle = 2.0 * np.pi * coarse[:, None] * order[None, :] / 512.0
    first = np.concatenate([np.cos(angle), -np.sin(angle)], 0)
    first_hi, first_lo = np_halves(first)
    w1 = np.concatenate([first_hi, first_hi, first_lo], 1)
    last_hi, last_lo = np_halves(first.T / length)
    w1t = np.concatenate([last_hi, last_hi, last_lo], 1)
    fine = np.arange(256)
    angle = 2.0 * np.pi * (fine[:, None] * fine[None, :] % 256) / 256.0
    cos, sin = np.cos(angle), np.sin(angle)
    mid_hi, mid_lo = np_halves(np.block([[cos, -sin], [sin, cos]]))
    w2 = np.concatenate([mid_hi, mid_hi, mid_lo], 0)
    back_hi, back_lo = np_halves(np.block([[cos, sin], [-sin, cos]]))
    w2c = np.concatenate([back_hi, back_hi, back_lo], 0)
    angle = 2.0 * np.pi * coarse[:, None] * fine[None, :] / points
    return w1, w1t, w2, w2c, np.cos(angle).astype(np.float32), -np.sin(angle).astype(np.float32)


def tile_rows(index, count):
    return pl.ds(pl.multiple_of(index * count, count), count)


def send(src, dst, send_sem, recv_sem, seq, ch):
    pltpu.make_async_remote_copy(
        src_ref=src,
        dst_ref=dst,
        send_sem=send_sem,
        recv_sem=recv_sem,
        device_id=(seq, ch),
        device_id_type=MESH,
    ).start()


def drain(ref, sem):
    pltpu.make_async_copy(ref, ref, sem).wait()


def greet(barrier, seq, ch):
    pl.semaphore_signal(barrier, inc=1, device_id=(seq, ch), device_id_type=MESH)


def inbound_kernel(
    msgb,
    hidden,
    readout,
    windows,
    inb,
    inh,
    feat,
    hbuf,
    f_send,
    f_recv,
    b_send,
    b_recv,
    h_send,
    h_recv,
):
    seq = lax.axis_index("seq")
    ch = lax.axis_index("ch")
    channel = lax.div(seq, 8)
    is_owner = owner_of(channel, ch) == seq
    barrier = pltpu.get_barrier_semaphore()
    for step in range(1, CH):
        greet(barrier, seq, lax.rem(ch + step, CH))

    @pl.when(is_owner)
    def _():
        @pl.loop(1, SEQ)
        def _(step):
            greet(barrier, lax.rem(seq + step, SEQ), ch)

        pl.semaphore_wait(barrier, WIDTH - 1 + CH - 1)

    @pl.when(jnp.logical_not(is_owner))
    def _():
        pl.semaphore_wait(barrier, WIDTH + CH - 1)

    mine = tile_rows(ch, WIDTH)
    for step in range(1, CH):
        send(hidden, feat.at[mine], f_send, f_recv, seq, lax.rem(ch + step, CH))
    feat[mine, :] = hidden[...]

    def spread(source, target, rows, send_sem, recv_sem):
        slot = tile_rows(seq, rows)

        @pl.loop(0, WIDTH)
        def _(step):
            to = lax.rem(channel + step, WIDTH)
            owner = owner_of(to, ch)
            piece = source.at[tile_rows(to, rows)]

            @pl.when(owner != seq)
            def _():
                send(piece, target.at[slot], send_sem, recv_sem, owner, ch)

            @pl.when(owner == seq)
            def _():
                pltpu.make_async_copy(piece, target.at[slot], recv_sem).start()

    spread(msgb, inb, 16, b_send, b_recv)
    drain(feat.at[pl.ds(0, 3 * WIDTH)], f_recv)
    filt = (
        jnp.dot(
            readout[...],
            feat[...].astype(F32),
            precision=lax.Precision.HIGHEST,
            preferred_element_type=F32,
        )
        * windows[...]
    )
    for order in range(2):
        for part in range(4):
            hbuf[pl.ds(order * 4 + part, WIDTH, stride=8), :] = filt[
                order * WIDTH : (order + 1) * WIDTH, part * 128 : (part + 1) * 128
            ]
    spread(hbuf, inh, 8, h_send, h_recv)
    drain(feat.at[pl.ds(0, 3 * WIDTH)], f_send)

    @pl.when(is_owner)
    def _():
        drain(msgb.at[pl.ds(0, (WIDTH - 1) * 16)], b_send)
        drain(hbuf.at[pl.ds(0, (WIDTH - 1) * 8)], h_send)
        drain(inb, b_recv)
        drain(inh, h_recv)

    @pl.when(jnp.logical_not(is_owner))
    def _():
        drain(msgb, b_send)
        drain(hbuf, h_send)


def channel_kernel(
    inb, inh, w1, w1t, w2, w2c, twr, twi, outb, outh, sbuf, dcat, ybuf, zcat, spec, qbuf, rcat, obuf
):
    seq = lax.axis_index("seq")
    ch = lax.axis_index("ch")

    def chunks(body):
        @pl.loop(0, 8)
        def _(step):
            body(pl.ds(pl.multiple_of(step * 32, 32), 32), step)

    def after(rows, base, step):
        return pl.ds(pl.multiple_of(base + step * 32, 32), 32)

    def put(ref, rows_list, columns_list, high, low):
        ref[rows_list[0], columns_list[0]] = high
        ref[rows_list[1], columns_list[1]] = low
        ref[rows_list[2], columns_list[2]] = high

    def forward(count, slot):
        width = 256 * count
        ybuf[:, pl.ds(0, width)] = jnp.dot(
            w1[...], dcat[:, pl.ds(0, width)], preferred_element_type=F32
        )
        for index in range(count):
            columns = pl.ds(index * 256, 256)

            def body(rows, step):
                re, im = ybuf[rows, columns], ybuf[after(rows, 256, step), columns]
                cr, ci = twr[rows, :], twi[rows, :]
                place = after(rows, index * 256, step)
                for base, value in ((0, re * cr - im * ci), (256, re * ci + im * cr)):
                    high, low = halves(value)
                    put(
                        zcat,
                        (place,) * 3,
                        tuple(pl.ds(base + 512 * k, 256) for k in range(3)),
                        high,
                        low,
                    )

            chunks(body)
        spec[pl.ds(slot * 256, width), :] = jnp.dot(
            zcat[pl.ds(0, width), :], w2[...], preferred_element_type=F32
        )

    def inverse(pairs):
        count = len(pairs)
        width = 256 * count
        for index, (left, right, conj) in enumerate(pairs):

            def body(rows, step):
                a, b = after(rows, left * 256, step), after(rows, right * 256, step)
                ar, ai = spec[a, pl.ds(0, 256)], spec[a, pl.ds(256, 256)]
                br, bi = spec[b, pl.ds(0, 256)], spec[b, pl.ds(256, 256)]
                if conj:
                    re, im = ar * br + ai * bi, ai * br - ar * bi
                else:
                    re, im = ar * br - ai * bi, ai * br + ar * bi
                place = after(rows, index * 256, step)
                for base, value in ((0, re), (256, im)):
                    high, low = halves(value)
                    put(
                        zcat,
                        (place,) * 3,
                        tuple(pl.ds(base + 512 * k, 256) for k in range(3)),
                        high,
                        low,
                    )

            chunks(body)
        qbuf[pl.ds(0, width), :] = jnp.dot(
            zcat[pl.ds(0, width), :], w2c[...], preferred_element_type=F32
        )
        for index in range(count):
            columns = pl.ds(index * 256, 256)

            def body(rows, step):
                place = after(rows, index * 256, step)
                re, im = qbuf[place, pl.ds(0, 256)], qbuf[place, pl.ds(256, 256)]
                cr, ci = twr[rows, :], twi[rows, :]
                for base, value in ((0, re * cr + im * ci), (256, im * cr - re * ci)):
                    high, low = halves(value)
                    put(
                        rcat,
                        tuple(after(rows, base + 512 * k, step) for k in range(3)),
                        (columns,) * 3,
                        high,
                        low,
                    )

            chunks(body)
        obuf[:, pl.ds(0, width)] = jnp.dot(
            w1t[...], rcat[:, pl.ds(0, width)], preferred_element_type=F32
        )

    def load(ref, stride, array, half):
        return jnp.concatenate(
            [
                ref[pl.ds(array * 4 + 2 * half + part, SEQ, stride=stride), :]
                for part in range(2)
            ],
            1,
        )

    def place(half, index, value):
        high, low = halves(value)
        put(
            dcat,
            tuple(pl.ds(256 * k + half * 128, 128) for k in range(3)),
            (pl.ds(index * 256, 256),) * 3,
            high,
            low,
        )

    def block(half, index):
        return obuf[pl.ds(half * 128, 128), pl.ds(index * 256, 256)]

    def store(ref, stride, array, half, value):
        for part in range(2):
            ref[pl.ds(array * 4 + 2 * half + part, SEQ, stride=stride), :] = value[
                :, part * 128 : (part + 1) * 128
            ]

    @pl.when(owner_of(lax.div(seq, 8), ch) == seq)
    def _():
        sbuf[...] = inb[...].astype(F32)
        for half in range(2):
            place(half, 0, load(sbuf, 16, 0, half))
            place(half, 1, load(inh, 8, 0, half))
            place(half, 2, load(sbuf, 16, 2, half) * load(sbuf, 16, 3, half))
            place(half, 3, load(inh, 8, 1, half))
        forward(4, 0)
        inverse(((0, 1, False), (2, 3, True)))
        for half in range(2):
            gate = load(sbuf, 16, 1, half)
            first_u, grad_z = block(half, 0), block(half, 1)
            place(half, 0, gate * first_u)
            place(half, 1, gate * grad_z)
            store(sbuf, 16, 1, half, first_u * grad_z)
        forward(2, 4)
        inverse(((5, 1, True), (4, 3, False), (5, 0, True), (2, 4, True)))
        for half in range(2):
            store(sbuf, 16, 0, half, block(half, 0))
            store(sbuf, 16, 2, half, load(sbuf, 16, 3, half) * block(half, 1))
            store(outh, 8, 0, half, block(half, 2))
            store(outh, 8, 1, half, block(half, 3))
        outb[...] = sbuf[...].astype(BF16)


def outbound_kernel(
    outb,
    outh,
    feat,
    readout,
    windows,
    gotb,
    hidden_out,
    readout_out,
    goth,
    part_f,
    got_f,
    part_w,
    got_w,
    sum_w,
    got_v,
    b_send,
    b_recv,
    h_send,
    h_recv,
    f_send,
    f_recv,
    w_send,
    w_recv,
    v_send,
    v_recv,
):
    seq = lax.axis_index("seq")
    ch = lax.axis_index("ch")
    channel = lax.div(seq, 8)
    low = lax.rem(seq, 8)
    is_owner = owner_of(channel, ch) == seq
    barrier = pltpu.get_barrier_semaphore()
    peers = CH - 1 + 15 + 7

    @pl.loop(0, WIDTH)
    def _(other):
        owner = owner_of(other, ch)

        @pl.when(owner != seq)
        def _():
            greet(barrier, owner, ch)

    for step in range(1, CH):
        greet(barrier, seq, lax.rem(ch + step, CH))

    @pl.loop(1, 16)
    def _(step):
        greet(barrier, lax.rem(channel + step, 16) * 8 + low, ch)

    @pl.loop(1, 8)
    def _(step):
        greet(barrier, channel * 8 + lax.rem(low + step, 8), ch)

    @pl.when(is_owner)
    def _():
        pl.semaphore_wait(barrier, SEQ - 1 + peers)

        @pl.loop(1, SEQ)
        def _(step):
            to = lax.rem(seq + step, SEQ)
            send(
                outh.at[tile_rows(to, 8)], goth.at[tile_rows(channel, 8)], h_send, h_recv, to, ch
            )

        @pl.loop(1, SEQ)
        def _(step):
            to = lax.rem(seq + step, SEQ)
            send(
                outb.at[tile_rows(to, 16)], gotb.at[tile_rows(channel, 16)], b_send, b_recv, to, ch
            )

        pltpu.make_async_copy(
            outh.at[tile_rows(seq, 8)], goth.at[tile_rows(channel, 8)], h_recv
        ).start()
        pltpu.make_async_copy(
            outb.at[tile_rows(seq, 16)], gotb.at[tile_rows(channel, 16)], b_recv
        ).start()

    @pl.when(jnp.logical_not(is_owner))
    def _():
        pl.semaphore_wait(barrier, peers)

    drain(goth, h_recv)
    rows = [
        jnp.concatenate(
            [goth[pl.ds(order * 4 + part, WIDTH, stride=8), :] for part in range(4)], 1
        )
        for order in range(2)
    ]
    dhw = jnp.concatenate(rows, 0) * windows[...] * (1.0 / math.sqrt(SEQ * LOCUS))
    full = feat[...].astype(F32)
    highest = lax.Precision.HIGHEST
    part_f[...] = lax.dot_general(
        readout[...], dhw, (((0,), (0,)), ((), ())), precision=highest, preferred_element_type=F32
    )
    for step in range(1, CH):
        to = lax.rem(ch + step, CH)
        send(
            part_f.at[tile_rows(to, WIDTH)], got_f.at[tile_rows(ch, WIDTH)], f_send, f_recv, seq, to
        )
    grads = lax.dot_general(
        dhw, full, (((1,), (1,)), ((), ())), precision=highest, preferred_element_type=F32
    )
    part_w[...] = jnp.concatenate([grads[:WIDTH], grads[WIDTH:]], 1)
    got_w[tile_rows(channel, 16), :] = part_w[...]
    got_f[tile_rows(ch, WIDTH), :] = part_f[tile_rows(ch, WIDTH), :]

    @pl.loop(1, 16)
    def _(step):
        to = lax.rem(channel + step, 16) * 8 + low
        send(part_w, got_w.at[tile_rows(channel, 16)], w_send, w_recv, to, ch)

    drain(got_w.at[pl.ds(0, 15 * 16)], w_recv)
    total = got_w[pl.ds(0, 16), :]
    for index in range(1, 16):
        total = total + got_w[pl.ds(16 * index, 16), :]
    sum_w[...] = total
    got_v[tile_rows(low, 16), :] = total

    @pl.loop(1, 8)
    def _(step):
        to = channel * 8 + lax.rem(low + step, 8)
        send(sum_w, got_v.at[tile_rows(low, 16)], v_send, v_recv, to, ch)

    drain(got_f.at[pl.ds(0, 3 * WIDTH)], f_recv)
    summed = got_f[pl.ds(0, WIDTH), :]
    for index in range(1, CH):
        summed = summed + got_f[pl.ds(WIDTH * index, WIDTH), :]
    hidden_out[...] = summed.astype(BF16)
    drain(got_v.at[pl.ds(0, 7 * 16)], v_recv)
    total = got_v[pl.ds(0, 16), :]
    for index in range(1, 8):
        total = total + got_v[pl.ds(16 * index, 16), :]
    readout_out[...] = total.astype(BF16)
    drain(gotb, b_recv)
    drain(got_f.at[pl.ds(0, 3 * WIDTH)], f_send)
    drain(got_w.at[pl.ds(0, 15 * 16)], w_send)
    drain(got_v.at[pl.ds(0, 7 * 16)], v_send)

    @pl.when(is_owner)
    def _():
        drain(outh.at[pl.ds(0, (SEQ - 1) * 8)], h_send)
        drain(outb.at[pl.ds(0, (SEQ - 1) * 16)], b_send)


def vmem(count):
    return [pl.BlockSpec(memory_space=pltpu.VMEM)] * count


def shape(dims, dtype):
    return jax.ShapeDtypeStruct(dims, dtype)


def params(collective):
    return pltpu.CompilerParams(
        collective_id=collective, has_side_effects=True, vmem_limit_bytes=48 * 2**20
    )


def channel_call(inb, inh):
    return pl.pallas_call(
        channel_kernel,
        out_shape=(shape((2048, 128), BF16), shape((1024, 128), F32)),
        in_specs=vmem(8),
        out_specs=tuple(vmem(2)),
        scratch_shapes=[
            pltpu.VMEM((2048, 128), F32),
            pltpu.VMEM((768, 1024), BF16),
            pltpu.VMEM((512, 1024), F32),
            pltpu.VMEM((1024, 1536), BF16),
            pltpu.VMEM((1536, 512), F32),
            pltpu.VMEM((1024, 512), F32),
            pltpu.VMEM((1536, 1024), BF16),
            pltpu.VMEM((256, 1024), F32),
        ],
        compiler_params=pltpu.CompilerParams(vmem_limit_bytes=48 * 2**20),
    )(inb, inh, *[jnp.asarray(table) for table in make_tables()])


def body(
    signal_branch,
    leading_multiplier,
    trailing_multiplier,
    loss_upstream_adjoint,
    kernel_net_hidden,
    kernel_readout_matrix,
    kernel_attenuation,
):
    dma = pltpu.SemaphoreType.DMA
    seq_index = lax.axis_index("seq")
    position = (seq_index * LOCUS + jnp.arange(LOCUS, dtype=jnp.int32)).astype(F32)
    window = jnp.exp(-kernel_attenuation[:, :, None] * position)
    scale = jnp.sqrt(
        jnp.expm1(-2.0 * kernel_attenuation) / jnp.expm1(-2.0 * kernel_attenuation * (SEQ * LOCUS))
    )
    windows = (window * scale[:, :, None]).reshape(2 * WIDTH, LOCUS)
    readout = kernel_readout_matrix.reshape(2 * WIDTH, CH * WIDTH)
    msgb = jnp.stack(
        [signal_branch, leading_multiplier, trailing_multiplier, loss_upstream_adjoint], 1
    ).reshape(WIDTH * 16, 128)
    inb, inh, feat = pl.pallas_call(
        inbound_kernel,
        out_shape=(shape((2048, 128), BF16), shape((1024, 128), F32), shape((64, LOCUS), BF16)),
        in_specs=vmem(4),
        out_specs=tuple(vmem(3)),
        scratch_shapes=[pltpu.VMEM((WIDTH * 8, 128), F32)] + [dma] * 6,
        compiler_params=params(1),
    )(msgb, kernel_net_hidden, readout, windows)
    outb, outh = channel_call(inb, inh)
    gotb, hidden_grad, readout_grad = pl.pallas_call(
        outbound_kernel,
        out_shape=(
            shape((WIDTH * 16, 128), BF16),
            shape((WIDTH, LOCUS), BF16),
            shape((WIDTH, 128), BF16),
        ),
        in_specs=vmem(5),
        out_specs=tuple(vmem(3)),
        scratch_shapes=[
            pltpu.VMEM((WIDTH * 8, 128), F32),
            pltpu.VMEM((64, LOCUS), F32),
            pltpu.VMEM((64, LOCUS), F32),
            pltpu.VMEM((16, 128), F32),
            pltpu.VMEM((256, 128), F32),
            pltpu.VMEM((16, 128), F32),
            pltpu.VMEM((128, 128), F32),
        ]
        + [dma] * 10,
        compiler_params=params(2),
    )(outb, outh, feat, readout, windows)
    pieces = gotb.reshape(WIDTH, 4, LOCUS)
    return (
        pieces[:, 0],
        pieces[:, 1],
        pieces[:, 2],
        readout_grad.reshape(WIDTH, 2, 64).transpose(1, 0, 2),
        hidden_grad,
    )


def solution(mesh):
    in_specs = (
        P("ch", "seq"),
        P("ch", "seq"),
        P("ch", "seq"),
        P("ch", "seq"),
        P("ch", "seq"),
        P(None, "ch", None),
        P(None, "ch"),
    )
    out_specs = (
        P("ch", "seq"),
        P("ch", "seq"),
        P("ch", "seq"),
        P(None, "ch", None),
        P("ch", "seq"),
    )
    return jax.shard_map(body, mesh=mesh, in_specs=in_specs, out_specs=out_specs, check_vma=False)
```

time: 1380 us -> 101 us (0.07)
  blocking collectives: 884 us -> 0 us
  waiting for transfers between devices: 248 us -> 0 us
  starting transfers between devices: 134 us -> 0 us
  Pallas kernels: 0 us -> 88.7 us
  matrix products: 34.2 us -> 0 us
  local copies, waits for them, and re-layouts: 32.3 us -> 9.88 us
  other arithmetic: 18.1 us -> 1.58 us
  between operations: 15.6 us -> 0.71 us
    psum x1 -> x0, blocking collectives: 790 us -> none  [body(): readout_adjoint_factored = lax.psum(partial_w, 'seq').astype(jnp.bfloat16)]
    all_to_all x15 -> x0, waiting for transfers between devices: 248 us -> none  [the longest x3 49.9 us: to_spectrum(): lax.all_to_all(real_z, 'seq', split_axis=3, concat_axis=3, tiled=True)]
    all_to_all x15 -> x0, starting transfers between devices: 134 us -> none  [the longest x3 28.2 us: from_spectrum(): lax.all_to_all(imag_a, 'seq', split_axis=3, concat_axis=3, tiled=True)]
    pallas_call x0 -> x3, Pallas kernels: none -> 88.7 us  [the longest x1 59.8 us: body(): pl.pallas_call(outbound_kernel, out_shape=(shape((WIDTH * 16, 128), BF16)...]
    all_to_all x3 -> x0, blocking collectives: 81.9 us -> none  [the longest x2 53.9 us: spectra(): lax.all_to_all(stack.reshape(stack.shape[0], slabs, seq_count), 'seq', sp...]
    dot_general x63 -> x0, matrix products: 34.2 us -> none  [the longest x3 2.37 us: to_spectrum(): real_y = jnp.einsum('xrq,qjd->xjrd', columns, cross_cos, precision=highest)]
    all_to_all x16 -> x0, other arithmetic: 15.1 us -> none  [the longest x3 2.89 us: to_spectrum(): lax.all_to_all(real_z, 'seq', split_axis=3, concat_axis=3, tiled=True)]
  transfers between devices with their start and end apart: 16 -> 0, of which waited for: 15 -> 0; matrix products, arithmetic and copies ran while one was open for 2% -> 0% of each run, Pallas kernels for 0% -> 0%
where the time goes in v1:
time: 101 us
  Pallas kernels  88.7 us (88%)
  local copies, waits for them, and re-layouts  9.88 us (10%)
  other arithmetic  1.58 us (2%)
    pallas_call x1, Pallas kernels, body(): pl.pallas_call(outbound_kernel, out_shape=(shape((WIDTH * 16, 128), BF16)...  59.8 us
    pallas_call x1, Pallas kernels, body(): pl.pallas_call(inbound_kernel, out_shape=(shape((2048, 128), BF16), shape...  27.5 us
    unnamed x18, local copies, waits for them, and re-layouts  8.22 us

profile of v1, /device:TPU:1, one launch (start us, length us, event | category | flops | bytes accessed | tf_op | source)
XLA Modules:
  0.0 100.9 jit_solution(13242448161121356268)
XLA Ops:
  0.6 0.7 fusion.2
  1.3 0.1 mul.40
  1.4 0.1 mul.48
  1.5 0.1 exponential_multiply_fusion.windows
  1.6 0.8 pad_maximum_fusion
  2.4 0.1 copy.18
  2.5 0.0 copy-start.5
  2.5 0.7 copy-done.5
  3.2 0.7 copy-done.7
  3.9 27.5 %shard_map.164 = (bf16[2048,128]{1,0:T(8,128)(2,1)S(1)}, f32[1024,128]{1,0:T(8,128)S(1)}, bf16[64,512]{1,0:T(8,128)(2,1)S(1)}) custom-call(bf16[256,128]{1,0:T(8,128)(2,1)S(1)} %reshape.35.msgb, bf16[16,512]{1,0:T(8,128)(2,1)S(1)} %copy-done.7, f32[32,64]{1,0:T(8,128)S(1)} %bitcast.15, f32[32,512]{1,0:T(8,128)S(1)} %exponential_multiply_fusion.windows), custom_call_target="tpu_custom_call" | custom-call | tf_op jit(solution)/shard_map/pallas_call | solution.py:523
  31.5 0.0 copy-start
  31.5 1.4 %copy-done = bf16[1536,512]{1,0:T(8,128)(2,1)S(1)} copy-done((bf16[1536,512]{1,0:T(8,128)(2,1)S(1)}, bf16[1536,512]{1,0:T(8,128)(2,1)}, u32[]{:S(2)}) %copy-start) | copy-done | bytes 1572888
  32.9 1.1 %copy-done.1 = bf16[256,1536]{1,0:T(8,128)(2,1)S(1)} copy-done((bf16[256,1536]{1,0:T(8,128)(2,1)S(1)}, bf16[256,1536]{1,0:T(8,128)(2,1)}, u32[]{:S(2)}) %copy-start.1) | copy-done | bytes 786456
  34.0 1.1 %copy-done.2 = bf16[512,768]{1,0:T(8,128)(2,1)S(1)} copy-done((bf16[512,768]{1,0:T(8,128)(2,1)S(1)}, bf16[512,768]{1,0:T(8,128)(2,1)}, u32[]{:S(2)}) %copy-start.2) | copy-done | bytes 786456
  35.2 0.9 copy-done.3
  36.1 0.9 copy-done.4
  37.1 1.4 %shard_map.165 = (bf16[2048,128]{1,0:T(8,128)(2,1)S(1)}, f32[1024,128]{1,0:T(8,128)S(1)}) custom-call(bf16[2048,128]{1,0:T(8,128)(2,1)S(1)} %get-tuple-element.13.inb, f32[1024,128]{1,0:T(8,128)S(1)} %get-tuple-element.14.inh, bf16[512,768]{1,0:T(8,128)(2,1)S(1)} %copy-done.2, bf16[256,1536]{1,0:T(8,128)(2,1)S(1)} %copy-done.1, ...), custom_call_target="tpu_custom_call" | custom-call | tf_op jit(solution)/shard_map/pallas_call | solution.py:483
  38.5 59.8 %shard_map.166 = (bf16[256,128]{1,0:T(8,128)(2,1)S(1)}, bf16[16,512]{1,0:T(8,128)(2,1)S(1)}, bf16[16,128]{1,0:T(8,128)(2,1)S(1)}) custom-call(bf16[2048,128]{1,0:T(8,128)(2,1)S(1)} %get-tuple-element.15.outb, f32[1024,128]{1,0:T(8,128)S(1)} %get-tuple-element.16.outh, bf16[64,512]{1,0:T(8,128)(2,1)S(1)} %get-tuple-element.17.feat, f32[32,64]{1,0:T(8,128)S(1)} %bitcast.16, ...), custom_call_target="tpu_custom_call" | custom-call | tf_op jit(solution)/shard_map/pallas_call | solution.py:532
  98.3 0.1 reshape.38
  98.4 0.6 copy.31
  99.0 0.1 fusion.1
  99.1 0.6 copy_bitcast_fusion
  99.7 0.6 copy.30
  100.3 0.6 copy.33
  (10 shorter events, 0.1 us)
Async XLA Ops:
  2.5 0.7 copy-start.5
  3.2 0.7 copy-start.7
  31.5 1.4 %copy-start = (bf16[1536,512]{1,0:T(8,128)(2,1)S(1)}, bf16[1536,512]{1,0:T(8,128)(2,1)}, u32[]{:S(2)}) copy-start(bf16[1536,512]{1,0:T(8,128)(2,1)} %constant.27.clone.w2) | copy-start | bytes 4718596
  32.9 1.1 %copy-start.1 = (bf16[256,1536]{1,0:T(8,128)(2,1)S(1)}, bf16[256,1536]{1,0:T(8,128)(2,1)}, u32[]{:S(2)}) copy-start(bf16[256,1536]{1,0:T(8,128)(2,1)} %constant.26.clone.w1t) | copy-start | bytes 2359300
  34.0 1.1 %copy-start.2 = (bf16[512,768]{1,0:T(8,128)(2,1)S(1)}, bf16[512,768]{1,0:T(8,128)(2,1)}, u32[]{:S(2)}) copy-start(bf16[512,768]{1,0:T(8,128)(2,1)} %constant.25.clone.w1) | copy-start | bytes 2359300
  35.2 0.9 copy-start.3
  36.1 0.9 copy-start.4
  37.1 1.4 %copy-start.6 = (f32[2,16,64]{2,1,0:T(8,128)S(1)}, f32[2,16,64]{2,1,0:T(8,128)}, u32[]{:S(2)}) copy-start(f32[2,16,64]{2,1,0:T(8,128)} %param.18) | copy-start | bytes 24580

commit v2 on v1

v2 whole, which is shorter than its diff:
```python
import math

import jax
import jax.numpy as jnp
import ml_dtypes
import numpy as np
from jax import lax
from jax.experimental import pallas as pl
from jax.experimental.pallas import tpu as pltpu
from jax.sharding import PartitionSpec as P

F32 = jnp.float32
BF16 = jnp.bfloat16
SEQ = 128
CH = 4
WIDTH = 16
LOCUS = 512
MESH = pl.DeviceIdType.MESH


def owner_of(channel, group):
    high = lax.rem(lax.div(channel, 4) + lax.rem(channel, 4) + group, 4)
    return channel * 8 + 2 * high


def halves(value):
    high = value.astype(BF16)
    return high, (value - high.astype(F32)).astype(BF16)


def np_halves(value):
    value = value.astype(np.float32)
    high = value.astype(ml_dtypes.bfloat16)
    return high, (value - high.astype(np.float32)).astype(ml_dtypes.bfloat16)


def make_tables():
    length = SEQ * LOCUS
    points = 2 * length
    order = np.concatenate([2 * np.arange(128), 2 * np.arange(128) + 1])
    coarse = np.arange(256) + 0.5
    angle = 2.0 * np.pi * coarse[:, None] * order[None, :] / 512.0
    first = np.concatenate([np.cos(angle), -np.sin(angle)], 0)
    first_hi, first_lo = np_halves(first)
    w1 = np.concatenate([first_hi, first_hi, first_lo], 1)
    last_hi, last_lo = np_halves(first.T / length)
    w1t = np.concatenate([last_hi, last_hi, last_lo], 1)
    fine = np.arange(256)
    angle = 2.0 * np.pi * (fine[:, None] * fine[None, :] % 256) / 256.0
    cos, sin = np.cos(angle), np.sin(angle)
    mid_hi, mid_lo = np_halves(np.block([[cos, -sin], [sin, cos]]))
    w2 = np.concatenate([mid_hi, mid_hi, mid_lo], 0)
    back_hi, back_lo = np_halves(np.block([[cos, sin], [-sin, cos]]))
    w2c = np.concatenate([back_hi, back_hi, back_lo], 0)
    angle = 2.0 * np.pi * coarse[:, None] * fine[None, :] / points
    return w1, w1t, w2, w2c, np.cos(angle).astype(np.float32), -np.sin(angle).astype(np.float32)


def tile_rows(index, count):
    return pl.ds(pl.multiple_of(index * count, count), count)


def send(src, dst, send_sem, recv_sem, seq, ch):
    pltpu.make_async_remote_copy(
        src_ref=src,
        dst_ref=dst,
        send_sem=send_sem,
        recv_sem=recv_sem,
        device_id=(seq, ch),
        device_id_type=MESH,
    ).start()


def drain(ref, sem):
    pltpu.make_async_copy(ref, ref, sem).wait()


def greet(barrier, seq, ch):
    pl.semaphore_signal(barrier, inc=1, device_id=(seq, ch), device_id_type=MESH)


def fused_kernel(
    branch,
    gate_a,
    gate_b,
    upstream,
    hidden,
    readout,
    windows,
    w1_hbm,
    w1t_hbm,
    w2_hbm,
    w2c_hbm,
    twr_hbm,
    twi_hbm,
    branch_out,
    gate_a_out,
    gate_b_out,
    readout_out,
    hidden_out,
    w1,
    w1t,
    w2,
    w2c,
    twr,
    twi,
    feat,
    stage,
    msg,
    inb,
    sbuf,
    gate,
    cross,
    dcat,
    ybuf,
    zcat,
    spec,
    qbuf,
    rcat,
    obuf,
    outb,
    got,
    part_f,
    got_f,
    part_w,
    got_w,
    sum_w,
    got_v,
    t_sem,
    f_send,
    f_recv,
    b_send,
    b_recv,
    g_send,
    g_recv,
    c_send,
    c_recv,
    s_send,
    s_recv,
    o_send,
    o_recv,
    p_send,
    p_recv,
    w_send,
    w_recv,
    v_send,
    v_recv,
):
    seq = lax.axis_index("seq")
    ch = lax.axis_index("ch")
    channel = lax.div(seq, 8)
    low = lax.rem(seq, 8)
    role = lax.rem(seq, 2)
    is_owner = owner_of(channel, ch) == seq - role
    partner = seq + 1 - 2 * role
    barrier = pltpu.get_barrier_semaphore()
    peers = CH - 1 + 15 + 7

    @pl.loop(0, WIDTH)
    def _(other):
        for core in range(2):
            owner = owner_of(other, ch) + core

            @pl.when(owner != seq)
            def _():
                greet(barrier, owner, ch)

    for step in range(1, CH):
        greet(barrier, seq, lax.rem(ch + step, CH))

    @pl.loop(1, 16)
    def _(step):
        greet(barrier, lax.rem(channel + step, 16) * 8 + low, ch)

    @pl.loop(1, 8)
    def _(step):
        greet(barrier, channel * 8 + lax.rem(low + step, 8), ch)

    tables = [
        (w1_hbm, w1),
        (w1t_hbm, w1t),
        (w2_hbm, w2),
        (w2c_hbm, w2c),
        (twr_hbm, twr),
        (twi_hbm, twi),
    ]

    @pl.when(is_owner)
    def _():
        @pl.loop(1, SEQ)
        def _(step):
            greet(barrier, lax.rem(seq + step, SEQ), ch)

        for index, (source, target) in enumerate(tables):
            pltpu.make_async_copy(source, target, t_sem.at[index]).start()

    def stage_rows(row, value):
        for part in range(4):
            stage[pl.ds(row + part, WIDTH, stride=16), :] = value[:, part * 128 : (part + 1) * 128]

    stage_rows(0, branch[...].astype(F32))
    stage_rows(4, gate_a[...].astype(F32))
    stage_rows(256, gate_b[...].astype(F32))
    stage_rows(260, upstream[...].astype(F32))

    @pl.when(is_owner)
    def _():
        pl.semaphore_wait(barrier, SEQ - 1 + 2 * WIDTH - 1 + peers)

    @pl.when(jnp.logical_not(is_owner))
    def _():
        pl.semaphore_wait(barrier, 2 * WIDTH + peers)

    mine = tile_rows(ch, WIDTH)
    for step in range(1, CH):
        send(hidden, feat.at[mine], f_send, f_recv, seq, lax.rem(ch + step, CH))
    feat[mine, :] = hidden[...]
    drain(feat.at[pl.ds(0, 3 * WIDTH)], f_recv)
    weight = readout[...]
    high, rest = halves(weight)
    middle, last = halves(weight - high.astype(F32))
    triple = jnp.dot(
        jnp.concatenate([high, middle, last], 0), feat[...], preferred_element_type=F32
    )
    filt = (triple[:32] + triple[32:64] + triple[64:]) * windows[...]
    for order in range(2):
        value = filt[order * WIDTH : (order + 1) * WIDTH]
        first = value.astype(BF16).astype(F32)
        stage_rows(order * 256 + 8, first)
        stage_rows(order * 256 + 12, value - first)
    msg[...] = stage[...].astype(BF16)
    slot = tile_rows(seq, 16)

    @pl.loop(0, WIDTH)
    def _(step):
        to = lax.rem(channel + step, WIDTH)
        for core in range(2):
            owner = owner_of(to, ch) + core
            piece = msg.at[tile_rows(core * WIDTH + to, 16)]

            @pl.when(owner != seq)
            def _():
                send(piece, inb.at[slot], b_send, b_recv, owner, ch)

            @pl.when(owner == seq)
            def _():
                pltpu.make_async_copy(piece, inb.at[slot], b_recv).start()

    def chunks(body):
        @pl.loop(0, 8)
        def _(step):
            body(pl.ds(pl.multiple_of(step * 32, 32), 32), step)

    def after(base, step):
        return pl.ds(pl.multiple_of(base + step * 32, 32), 32)

    def put_rows(place, base, value):
        high, low = halves(value)
        zcat[place, pl.ds(base, 256)] = high
        zcat[place, pl.ds(base + 512, 256)] = low
        zcat[place, pl.ds(base + 1024, 256)] = high

    def forward(count, slot):
        width = 256 * count
        ybuf[:, pl.ds(0, width)] = jnp.dot(
            w1[...], dcat[:, pl.ds(0, width)], preferred_element_type=F32
        )
        for index in range(count):
            columns = pl.ds(index * 256, 256)

            def body(rows, step):
                re, im = ybuf[rows, columns], ybuf[after(256, step), columns]
                cr, ci = twr[rows, :], twi[rows, :]
                place = after(index * 256, step)
                put_rows(place, 0, re * cr - im * ci)
                put_rows(place, 256, re * ci + im * cr)

            chunks(body)
        spec[pl.ds(slot * 256, width), :] = jnp.dot(
            zcat[pl.ds(0, width), :], w2[...], preferred_element_type=F32
        )

    def inverse(pairs):
        count = len(pairs)
        width = 256 * count
        for index, (left, right, sign, flip) in enumerate(pairs):

            def body(rows, step):
                a, b = after(left * 256, step), after(right * 256, step)
                ar, ai = spec[a, pl.ds(0, 256)], spec[a, pl.ds(256, 256)]
                br, bi = spec[b, pl.ds(0, 256)], spec[b, pl.ds(256, 256)] * sign
                place = after(index * 256, step)
                put_rows(place, 0, ar * br - ai * bi)
                put_rows(place, 256, (ar * bi + ai * br) * flip)

            chunks(body)
        qbuf[pl.ds(0, width), :] = jnp.dot(
            zcat[pl.ds(0, width), :], w2c[...], preferred_element_type=F32
        )
        for index in range(count):
            columns = pl.ds(index * 256, 256)

            def body(rows, step):
                place = after(index * 256, step)
                re, im = qbuf[place, pl.ds(0, 256)], qbuf[place, pl.ds(256, 256)]
                cr, ci = twr[rows, :], twi[rows, :]
                for base, value in ((0, re * cr + im * ci), (256, im * cr - re * ci)):
                    high, low = halves(value)
                    rcat[after(base, step), columns] = high
                    rcat[after(base + 512, step), columns] = low
                    rcat[after(base + 1024, step), columns] = high

            chunks(body)
        obuf[:, pl.ds(0, width)] = jnp.dot(
            w1t[...], rcat[:, pl.ds(0, width)], preferred_element_type=F32
        )

    def load(array, half):
        return jnp.concatenate(
            [sbuf[pl.ds(array * 4 + 2 * half + part, SEQ, stride=16), :] for part in range(2)], 1
        )

    def store(array, half, value):
        for part in range(2):
            sbuf[pl.ds(array * 4 + 2 * half + part, SEQ, stride=16), :] = value[
                :, part * 128 : (part + 1) * 128
            ]

    def place(half, index, high, low):
        columns = pl.ds(index * 256, 256)
        dcat[pl.ds(half * 128, 128), columns] = high
        dcat[pl.ds(256 + half * 128, 128), columns] = low
        dcat[pl.ds(512 + half * 128, 128), columns] = high

    def block(half, index):
        return obuf[pl.ds(half * 128, 128), pl.ds(index * 256, 256)]

    def swap(source, target, send_sem, recv_sem):
        return pltpu.make_async_remote_copy(
            src_ref=source,
            dst_ref=target,
            send_sem=send_sem,
            recv_sem=recv_sem,
            device_id=(partner, ch),
            device_id_type=MESH,
        )

    @pl.when(is_owner)
    def _():
        for index, (source, target) in enumerate(tables):
            pltpu.make_async_copy(source, target, t_sem.at[index]).wait()
        drain(inb, b_recv)
        first_core = role == 0
        sign = jnp.where(first_core, 1.0, -1.0).astype(F32)
        sbuf[...] = inb[...].astype(F32)
        for half in range(2):
            second = load(1, half)
            rows = pl.ds(half * 128, 128)
            place(half, 0, *halves(load(0, half) * jnp.where(first_core, 1.0, second)))
            place(half, 1, load(2, half).astype(BF16), load(3, half).astype(BF16))

            @pl.when(first_core)
            def _():
                gate[rows, :] = second

        @pl.when(first_core)
        def _():
            swap(gate, gate, g_send, g_recv).start()

        forward(2, 0)
        inverse(((0, 1, sign, 1.0),))

        @pl.when(first_core)
        def _():
            drain(gate, g_send)

        @pl.when(jnp.logical_not(first_core))
        def _():
            drain(gate, g_recv)

        for half in range(2):
            rows = pl.ds(half * 128, 128)
            value = block(half, 0)
            place(half, 0, *halves(gate[rows, :] * value))

            @pl.when(first_core)
            def _():
                store(3, half, value)

            @pl.when(jnp.logical_not(first_core))
            def _():
                cross[rows, :] = value

        @pl.when(jnp.logical_not(first_core))
        def _():
            swap(cross, cross, c_send, c_recv).start()

        forward(1, 2)
        mine = pl.ds(512, 256)
        theirs = pl.ds(768, 256)
        copy = swap(spec.at[mine], spec.at[theirs], s_send, s_recv)
        copy.start()
        copy.wait()
        inverse(((3, 1, -sign, 1.0), (3, 0, -1.0, sign)))

        @pl.when(first_core)
        def _():
            drain(cross, c_recv)
            for half in range(2):
                store(0, half, block(half, 0))
                store(1, half, load(3, half) * cross[pl.ds(half * 128, 128), :])

        @pl.when(jnp.logical_not(first_core))
        def _():
            drain(cross, c_send)
            for half in range(2):
                store(0, half, block(half, 0) * load(1, half))

        for half in range(2):
            value = block(half, 1)
            first = value.astype(BF16).astype(F32)
            store(2, half, first)
            store(3, half, value - first)
        outb[...] = sbuf[...].astype(BF16)
        home = tile_rows(role * WIDTH + channel, 16)

        @pl.loop(1, SEQ)
        def _(step):
            to = lax.rem(seq + step, SEQ)
            send(outb.at[tile_rows(to, 16)], got.at[home], o_send, o_recv, to, ch)

        pltpu.make_async_copy(outb.at[slot], got.at[home], o_recv).start()

    drain(got, o_recv)
    stage[...] = got[...].astype(F32)

    def taken(row):
        return jnp.concatenate(
            [stage[pl.ds(row + part, WIDTH, stride=16), :] for part in range(4)], 1
        )

    grads = jnp.concatenate([taken(8) + taken(12), taken(264) + taken(268)], 0)
    dhw = grads * windows[...] * (1.0 / math.sqrt(SEQ * LOCUS))
    dhi, dlo = halves(dhw)
    whi, wlo = high, middle
    part_f[...] = lax.dot_general(
        jnp.concatenate([whi, whi, wlo], 0),
        jnp.concatenate([dhi, dlo, dhi], 0),
        (((0,), (0,)), ((), ())),
        preferred_element_type=F32,
    )
    double = lax.dot_general(
        jnp.concatenate([dhi, dlo], 0),
        feat[...],
        (((1,), (1,)), ((), ())),
        preferred_element_type=F32,
    )
    total = double[:32] + double[32:]
    part_w[...] = jnp.concatenate([total[:WIDTH], total[WIDTH:]], 1)

    @pl.loop(1, 16)
    def _(step):
        to = lax.rem(channel + step, 16) * 8 + low
        send(part_w, got_w.at[tile_rows(channel, 16)], w_send, w_recv, to, ch)

    for step in range(1, CH):
        to = lax.rem(ch + step, CH)
        send(part_f.at[tile_rows(to, WIDTH)], got_f.at[mine], p_send, p_recv, seq, to)
    got_w[tile_rows(channel, 16), :] = part_w[...]
    got_f[mine, :] = part_f[mine, :]
    branch_out[...] = taken(0).astype(BF16)
    gate_a_out[...] = taken(4).astype(BF16)
    gate_b_out[...] = taken(256).astype(BF16)
    drain(got_w.at[pl.ds(0, 15 * 16)], w_recv)
    total = got_w[pl.ds(0, 16), :]
    for index in range(1, 16):
        total = total + got_w[pl.ds(16 * index, 16), :]
    sum_w[...] = total

    @pl.loop(1, 8)
    def _(step):
        to = channel * 8 + lax.rem(low + step, 8)
        send(sum_w, got_v.at[tile_rows(low, 16)], v_send, v_recv, to, ch)

    got_v[tile_rows(low, 16), :] = total
    drain(got_f.at[pl.ds(0, 3 * WIDTH)], p_recv)
    summed = got_f[pl.ds(0, WIDTH), :]
    for index in range(1, CH):
        summed = summed + got_f[pl.ds(WIDTH * index, WIDTH), :]
    hidden_out[...] = summed.astype(BF16)
    drain(feat.at[pl.ds(0, 3 * WIDTH)], f_send)
    drain(got_f.at[pl.ds(0, 3 * WIDTH)], p_send)
    drain(got_w.at[pl.ds(0, 15 * 16)], w_send)

    @pl.when(is_owner)
    def _():
        drain(msg.at[pl.ds(0, (2 * WIDTH - 1) * 16)], b_send)
        drain(outb.at[pl.ds(0, (SEQ - 1) * 16)], o_send)

    @pl.when(jnp.logical_not(is_owner))
    def _():
        drain(msg, b_send)

    drain(got_v.at[pl.ds(0, 7 * 16)], v_recv)
    total = got_v[pl.ds(0, 16), :]
    for index in range(1, 8):
        total = total + got_v[pl.ds(16 * index, 16), :]
    readout_out[...] = total.astype(BF16)
    drain(got_v.at[pl.ds(0, 7 * 16)], v_send)


def vmem(count):
    return [pl.BlockSpec(memory_space=pltpu.VMEM)] * count


def shape(dims, dtype):
    return jax.ShapeDtypeStruct(dims, dtype)


def body(
    signal_branch,
    leading_multiplier,
    trailing_multiplier,
    loss_upstream_adjoint,
    kernel_net_hidden,
    kernel_readout_matrix,
    kernel_attenuation,
):
    dma = pltpu.SemaphoreType.DMA
    seq_index = lax.axis_index("seq")
    position = (seq_index * LOCUS + jnp.arange(LOCUS, dtype=jnp.int32)).astype(F32)
    window = jnp.exp(-kernel_attenuation[:, :, None] * position)
    scale = jnp.sqrt(
        jnp.expm1(-2.0 * kernel_attenuation) / jnp.expm1(-2.0 * kernel_attenuation * (SEQ * LOCUS))
    )
    windows = (window * scale[:, :, None]).reshape(2 * WIDTH, LOCUS)
    readout = kernel_readout_matrix.reshape(2 * WIDTH, CH * WIDTH)
    tables = [jnp.asarray(table) for table in make_tables()]
    rows = shape((WIDTH, LOCUS), BF16)
    dv, da, db, readout_grad, hidden_grad = pl.pallas_call(
        fused_kernel,
        out_shape=(rows, rows, rows, shape((WIDTH, 128), BF16), rows),
        in_specs=vmem(7) + [pl.BlockSpec(memory_space=pl.ANY)] * 6,
        out_specs=tuple(vmem(5)),
        scratch_shapes=[pltpu.VMEM(table.shape, table.dtype) for table in tables]
        + [
            pltpu.VMEM((64, LOCUS), BF16),
            pltpu.VMEM((512, 128), F32),
            pltpu.VMEM((512, 128), BF16),
            pltpu.VMEM((2048, 128), BF16),
            pltpu.VMEM((2048, 128), F32),
            pltpu.VMEM((256, 256), F32),
            pltpu.VMEM((256, 256), F32),
            pltpu.VMEM((768, 512), BF16),
            pltpu.VMEM((512, 512), F32),
            pltpu.VMEM((512, 1536), BF16),
            pltpu.VMEM((1024, 512), F32),
            pltpu.VMEM((512, 512), F32),
            pltpu.VMEM((1536, 512), BF16),
            pltpu.VMEM((256, 512), F32),
            pltpu.VMEM((2048, 128), BF16),
            pltpu.VMEM((512, 128), BF16),
            pltpu.VMEM((64, LOCUS), F32),
            pltpu.VMEM((64, LOCUS), F32),
            pltpu.VMEM((16, 128), F32),
            pltpu.VMEM((256, 128), F32),
            pltpu.VMEM((16, 128), F32),
            pltpu.VMEM((128, 128), F32),
            pltpu.SemaphoreType.DMA((6,)),
        ]
        + [dma] * 18,
        compiler_params=pltpu.CompilerParams(
            collective_id=1, has_side_effects=True, vmem_limit_bytes=48 * 2**20
        ),
    )(
        signal_branch,
        leading_multiplier,
        trailing_multiplier,
        loss_upstream_adjoint,
        kernel_net_hidden,
        readout,
        windows,
        *tables,
    )
    return (dv, da, db, readout_grad.reshape(WIDTH, 2, 64).transpose(1, 0, 2), hidden_grad)


def solution(mesh):
    in_specs = (
        P("ch", "seq"),
        P("ch", "seq"),
        P("ch", "seq"),
        P("ch", "seq"),
        P("ch", "seq"),
        P(None, "ch", None),
        P(None, "ch"),
    )
    out_specs = (
        P("ch", "seq"),
        P("ch", "seq"),
        P("ch", "seq"),
        P(None, "ch", None),
        P("ch", "seq"),
    )
    return jax.shard_map(body, mesh=mesh, in_specs=in_specs, out_specs=out_specs, check_vma=False)
```

time: 101 us -> 93.8 us (0.929)
  Pallas kernels: 88.7 us -> 77.1 us
  local copies, waits for them, and re-layouts: 9.88 us -> 14.5 us
    pallas_call x3 -> x1, Pallas kernels: 88.7 us -> 77.1 us  [body(): pl.pallas_call(fused_kernel, out_shape=(rows, rows, rows, shape((WIDTH, 1...]
    unnamed x18 -> x28, local copies, waits for them, and re-layouts: 8.22 us -> 13.7 us
where the time goes in v2:
time: 93.8 us; the launch traced here: 93.2 us
  Pallas kernels  77.1 us (82%)
  local copies, waits for them, and re-layouts  14.5 us (15%)
    pallas_call x1, Pallas kernels, body(): pl.pallas_call(fused_kernel, out_shape=(rows, rows, rows, shape((WIDTH, 1...  77.1 us
    unnamed x28, local copies, waits for them, and re-layouts  13.7 us

profile of v2, /device:TPU:1, one launch (start us, length us, event | category | flops | bytes accessed | tf_op | source)
XLA Modules:
  0.0 93.2 jit_solution(18127466381917122049)
XLA Ops:
  0.6 0.7 fusion.1
  1.3 0.1 mul.40
  1.4 0.1 mul.48
  1.5 0.1 exponential_multiply_fusion.windows
  1.6 0.0 copy-start
  1.6 1.4 %copy-done = bf16[1536,512]{1,0:T(8,128)(2,1)S(1)} copy-done((bf16[1536,512]{1,0:T(8,128)(2,1)S(1)}, bf16[1536,512]{1,0:T(8,128)(2,1)}, u32[]{:S(2)}) %copy-start) | copy-done | bytes 1572888
  3.0 1.4 %copy-done.1 = bf16[1536,512]{1,0:T(8,128)(2,1)S(1)} copy-done((bf16[1536,512]{1,0:T(8,128)(2,1)S(1)}, bf16[1536,512]{1,0:T(8,128)(2,1)}, u32[]{:S(2)}) %copy-start.1) | copy-done | bytes 1572888
  4.4 1.1 %copy-done.2 = bf16[256,1536]{1,0:T(8,128)(2,1)S(1)} copy-done((bf16[256,1536]{1,0:T(8,128)(2,1)S(1)}, bf16[256,1536]{1,0:T(8,128)(2,1)}, u32[]{:S(2)}) %copy-start.2) | copy-done | bytes 786456
  5.6 1.1 %copy-done.3 = bf16[512,768]{1,0:T(8,128)(2,1)S(1)} copy-done((bf16[512,768]{1,0:T(8,128)(2,1)S(1)}, bf16[512,768]{1,0:T(8,128)(2,1)}, u32[]{:S(2)}) %copy-start.3) | copy-done | bytes 786456
  6.7 0.9 %copy-done.4 = f32[256,256]{1,0:T(8,128)S(1)} copy-done((f32[256,256]{1,0:T(8,128)S(1)}, f32[256,256]{1,0:T(8,128)}, u32[]{:S(2)}) %copy-start.4) | copy-done | bytes 262168
  7.7 0.9 %copy-done.5 = f32[256,256]{1,0:T(8,128)S(1)} copy-done((f32[256,256]{1,0:T(8,128)S(1)}, f32[256,256]{1,0:T(8,128)}, u32[]{:S(2)}) %copy-start.5) | copy-done | bytes 262168
  8.6 0.7 copy-done.6
  9.3 0.7 copy-done.7
  10.0 0.7 copy-done.8
  10.8 0.7 copy-done.9
  11.5 0.7 copy-done.10
  12.2 0.7 copy-done.11
  12.9 77.1 %shard_map.164 = (bf16[16,512]{1,0:T(8,128)(2,1)S(1)}, bf16[16,512]{1,0:T(8,128)(2,1)S(1)}, bf16[16,512]{1,0:T(8,128)(2,1)S(1)}, bf16[16,128]{1,0:T(8,128)(2,1)S(1)}, bf16[16,512]{1,0:T(8,128)(2,1)S(1)}) custom-call(bf16[16,512]{1,0:T(8,128)(2,1)S(1)} %copy-done.6, bf16[16,512]{1,0:T(8,128)(2,1)S(1)} %copy-done.7, bf16[16,512]{1,0:T(8,128)(2,1)S(1)} %copy-done.8, ...), custom_call_target="tpu_custom_call" | custom-call | tf_op jit(solution)/shard_map/pallas_call | solution.py:540
  90.1 0.1 reshape.30
  90.1 0.6 copy.20
  90.7 0.6 copy.25
  91.3 0.6 copy.26
  92.0 0.6 copy.27
  92.6 0.6 copy.28
  (12 shorter events, 0.0 us)
Async XLA Ops:
  1.6 1.4 %copy-start = (bf16[1536,512]{1,0:T(8,128)(2,1)S(1)}, bf16[1536,512]{1,0:T(8,128)(2,1)}, u32[]{:S(2)}) copy-start(bf16[1536,512]{1,0:T(8,128)(2,1)} %constant.28.clone.w2c_hbm) | copy-start | bytes 4718596
  3.0 1.4 %copy-start.1 = (bf16[1536,512]{1,0:T(8,128)(2,1)S(1)}, bf16[1536,512]{1,0:T(8,128)(2,1)}, u32[]{:S(2)}) copy-start(bf16[1536,512]{1,0:T(8,128)(2,1)} %constant.27.clone.w2_hbm) | copy-start | bytes 4718596
  4.4 1.1 %copy-start.2 = (bf16[256,1536]{1,0:T(8,128)(2,1)S(1)}, bf16[256,1536]{1,0:T(8,128)(2,1)}, u32[]{:S(2)}) copy-start(bf16[256,1536]{1,0:T(8,128)(2,1)} %constant.26.clone.w1t_hbm) | copy-start | bytes 2359300
  5.6 1.1 %copy-start.3 = (bf16[512,768]{1,0:T(8,128)(2,1)S(1)}, bf16[512,768]{1,0:T(8,128)(2,1)}, u32[]{:S(2)}) copy-start(bf16[512,768]{1,0:T(8,128)(2,1)} %constant.25.clone.w1_hbm) | copy-start | bytes 2359300
  6.7 0.9 %copy-start.4 = (f32[256,256]{1,0:T(8,128)S(1)}, f32[256,256]{1,0:T(8,128)}, u32[]{:S(2)}) copy-start(f32[256,256]{1,0:T(8,128)} %constant.30.clone.twi_hbm) | copy-start | bytes 786436
  7.6 0.9 %copy-start.5 = (f32[256,256]{1,0:T(8,128)S(1)}, f32[256,256]{1,0:T(8,128)}, u32[]{:S(2)}) copy-start(f32[256,256]{1,0:T(8,128)} %constant.29.clone.twr_hbm) | copy-start | bytes 786436
  8.6 0.7 copy-start.6
  9.3 0.7 copy-start.7
  10.0 0.7 copy-start.8
  10.8 0.7 copy-start.9
  11.5 0.7 copy-start.10
  12.2 0.7 copy-start.11

commit v3 on v2

--- a/solution.py
+++ b/solution.py
@@ -15,12 +15,20 @@
 CH = 4
 WIDTH = 16
 LOCUS = 512
+VMEM_BYTES = 60 * 2**20
 MESH = pl.DeviceIdType.MESH
 
 
 def owner_of(channel, group):
-    high = lax.rem(lax.div(channel, 4) + lax.rem(channel, 4) + group, 4)
+    high = lax.rem(lax.div(channel, 4) + lax.rem(channel, 4) + 3 * group, 4)
     return channel * 8 + 2 * high
+
+
+def less_one(value):
+    near = jnp.ones_like(value)
+    for term in range(11, 1, -1):
+        near = 1.0 + near * value * (1.0 / term)
+    return jnp.where(jnp.abs(value) < 0.5, near * value, jnp.exp(value) - 1.0)
 
 
 def halves(value):
@@ -80,30 +88,33 @@
 
 
 def fused_kernel(
-    branch,
-    gate_a,
-    gate_b,
-    upstream,
+    branch_hbm,
+    gate_a_hbm,
+    gate_b_hbm,
+    upstream_hbm,
     hidden,
-    readout,
-    windows,
+    readout_hbm,
+    decay_hbm,
     w1_hbm,
     w1t_hbm,
     w2_hbm,
     w2c_hbm,
     twr_hbm,
     twi_hbm,
-    branch_out,
-    gate_a_out,
-    gate_b_out,
-    readout_out,
-    hidden_out,
+    packed,
     w1,
     w1t,
     w2,
     w2c,
     twr,
     twi,
+    branch,
+    gate_a,
+    gate_b,
+    upstream,
+    readout,
+    decay,
+    windows,
     feat,
     stage,
     msg,
@@ -127,6 +138,7 @@
     sum_w,
     got_v,
     t_sem,
+    a_sem,
     f_send,
     f_recv,
     b_send,
@@ -154,27 +166,22 @@
     is_owner = owner_of(channel, ch) == seq - role
     partner = seq + 1 - 2 * role
     barrier = pltpu.get_barrier_semaphore()
-    peers = CH - 1 + 15 + 7
-
-    @pl.loop(0, WIDTH)
-    def _(other):
-        for core in range(2):
-            owner = owner_of(other, ch) + core
-
-            @pl.when(owner != seq)
-            def _():
-                greet(barrier, owner, ch)
+    mine = tile_rows(ch, WIDTH)
 
     for step in range(1, CH):
         greet(barrier, seq, lax.rem(ch + step, CH))
 
-    @pl.loop(1, 16)
-    def _(step):
-        greet(barrier, lax.rem(channel + step, 16) * 8 + low, ch)
-
-    @pl.loop(1, 8)
-    def _(step):
-        greet(barrier, channel * 8 + lax.rem(low + step, 8), ch)
+    arguments = [
+        (hidden, feat.at[mine]),
+        (branch_hbm, branch),
+        (gate_a_hbm, gate_a),
+        (gate_b_hbm, gate_b),
+        (upstream_hbm, upstream),
+        (readout_hbm, readout),
+        (decay_hbm, decay),
+    ]
+    for index, (source, target) in enumerate(arguments):
+        pltpu.make_async_copy(source, target, a_sem.at[index]).start()
 
     tables = [
         (w1_hbm, w1),
@@ -198,23 +205,39 @@
         for part in range(4):
             stage[pl.ds(row + part, WIDTH, stride=16), :] = value[:, part * 128 : (part + 1) * 128]
 
+    for index, (source, target) in enumerate(arguments):
+        pltpu.make_async_copy(source, target, a_sem.at[index]).wait()
     stage_rows(0, branch[...].astype(F32))
     stage_rows(4, gate_a[...].astype(F32))
     stage_rows(256, gate_b[...].astype(F32))
     stage_rows(260, upstream[...].astype(F32))
+    rate = decay[...]
+    scale = jnp.sqrt(less_one(-2.0 * rate) / less_one(-2.0 * rate * (SEQ * LOCUS)))
+    diagonal = lax.broadcasted_iota(jnp.int32, (WIDTH, WIDTH), 0) == lax.broadcasted_iota(
+        jnp.int32, (WIDTH, WIDTH), 1
+    )
+    position = (
+        seq * LOCUS + lax.broadcasted_iota(jnp.int32, (WIDTH, LOCUS), 1)
+    ).astype(F32)
+
+    def column(values, order):
+        return jnp.sum(jnp.where(diagonal, values[order : order + 1], 0.0), 1, keepdims=True)
+
+    for order in range(2):
+        windows[pl.ds(order * WIDTH, WIDTH), :] = jnp.exp(
+            -column(rate, order) * position
+        ) * column(scale, order)
 
     @pl.when(is_owner)
     def _():
-        pl.semaphore_wait(barrier, SEQ - 1 + 2 * WIDTH - 1 + peers)
+        pl.semaphore_wait(barrier, 2 * WIDTH - 1 + CH - 1)
 
     @pl.when(jnp.logical_not(is_owner))
     def _():
-        pl.semaphore_wait(barrier, 2 * WIDTH + peers)
-
-    mine = tile_rows(ch, WIDTH)
+        pl.semaphore_wait(barrier, 2 * WIDTH + CH - 1)
+
     for step in range(1, CH):
         send(hidden, feat.at[mine], f_send, f_recv, seq, lax.rem(ch + step, CH))
-    feat[mine, :] = hidden[...]
     drain(feat.at[pl.ds(0, 3 * WIDTH)], f_recv)
     weight = readout[...]
     high, rest = halves(weight)
@@ -468,9 +491,9 @@
         send(part_f.at[tile_rows(to, WIDTH)], got_f.at[mine], p_send, p_recv, seq, to)
     got_w[tile_rows(channel, 16), :] = part_w[...]
     got_f[mine, :] = part_f[mine, :]
-    branch_out[...] = taken(0).astype(BF16)
-    gate_a_out[...] = taken(4).astype(BF16)
-    gate_b_out[...] = taken(256).astype(BF16)
+    packed[pl.ds(0, WIDTH), :] = taken(0).astype(BF16)
+    packed[pl.ds(16, WIDTH), :] = taken(4).astype(BF16)
+    packed[pl.ds(32, WIDTH), :] = taken(256).astype(BF16)
     drain(got_w.at[pl.ds(0, 15 * 16)], w_recv)
     total = got_w[pl.ds(0, 16), :]
     for index in range(1, 16):
@@ -487,7 +510,7 @@
     summed = got_f[pl.ds(0, WIDTH), :]
     for index in range(1, CH):
         summed = summed + got_f[pl.ds(WIDTH * index, WIDTH), :]
-    hidden_out[...] = summed.astype(BF16)
+    packed[pl.ds(48, WIDTH), :] = summed.astype(BF16)
     drain(feat.at[pl.ds(0, 3 * WIDTH)], f_send)
     drain(got_f.at[pl.ds(0, 3 * WIDTH)], p_send)
     drain(got_w.at[pl.ds(0, 15 * 16)], w_send)
@@ -505,7 +528,7 @@
     total = got_v[pl.ds(0, 16), :]
     for index in range(1, 8):
         total = total + got_v[pl.ds(16 * index, 16), :]
-    readout_out[...] = total.astype(BF16)
+    packed[pl.ds(64, 2 * WIDTH), pl.ds(0, 64)] = jnp.concatenate([total[:, :64], total[:, 64:]], 0).astype(BF16)
     drain(got_v.at[pl.ds(0, 7 * 16)], v_send)
 
 
@@ -527,23 +550,19 @@
     kernel_attenuation,
 ):
     dma = pltpu.SemaphoreType.DMA
-    seq_index = lax.axis_index("seq")
-    position = (seq_index * LOCUS + jnp.arange(LOCUS, dtype=jnp.int32)).astype(F32)
-    window = jnp.exp(-kernel_attenuation[:, :, None] * position)
-    scale = jnp.sqrt(
-        jnp.expm1(-2.0 * kernel_attenuation) / jnp.expm1(-2.0 * kernel_attenuation * (SEQ * LOCUS))
-    )
-    windows = (window * scale[:, :, None]).reshape(2 * WIDTH, LOCUS)
     readout = kernel_readout_matrix.reshape(2 * WIDTH, CH * WIDTH)
     tables = [jnp.asarray(table) for table in make_tables()]
-    rows = shape((WIDTH, LOCUS), BF16)
-    dv, da, db, readout_grad, hidden_grad = pl.pallas_call(
+    packed = pl.pallas_call(
         fused_kernel,
-        out_shape=(rows, rows, rows, shape((WIDTH, 128), BF16), rows),
-        in_specs=vmem(7) + [pl.BlockSpec(memory_space=pl.ANY)] * 6,
-        out_specs=tuple(vmem(5)),
+        out_shape=shape((96, LOCUS), BF16),
+        in_specs=[pl.BlockSpec(memory_space=pltpu.HBM)] * 13,
+        out_specs=vmem(1)[0],
         scratch_shapes=[pltpu.VMEM(table.shape, table.dtype) for table in tables]
+        + [pltpu.VMEM((WIDTH, LOCUS), BF16)] * 4
         + [
+            pltpu.VMEM((2 * WIDTH, 64), F32),
+            pltpu.VMEM((2, WIDTH), F32),
+            pltpu.VMEM((2 * WIDTH, LOCUS), F32),
             pltpu.VMEM((64, LOCUS), BF16),
             pltpu.VMEM((512, 128), F32),
             pltpu.VMEM((512, 128), BF16),
@@ -567,10 +586,11 @@
             pltpu.VMEM((16, 128), F32),
             pltpu.VMEM((128, 128), F32),
             pltpu.SemaphoreType.DMA((6,)),
+            pltpu.SemaphoreType.DMA((7,)),
         ]
         + [dma] * 18,
         compiler_params=pltpu.CompilerParams(
-            collective_id=1, has_side_effects=True, vmem_limit_bytes=48 * 2**20
+            collective_id=1, has_side_effects=True, vmem_limit_bytes=VMEM_BYTES
         ),
     )(
         signal_branch,
@@ -579,10 +599,16 @@
         loss_upstream_adjoint,
         kernel_net_hidden,
         readout,
-        windows,
+        kernel_attenuation,
         *tables,
     )
-    return (dv, da, db, readout_grad.reshape(WIDTH, 2, 64).transpose(1, 0, 2), hidden_grad)
+    return (
+        packed[:16],
+        packed[16:32],
+        packed[32:48],
+        packed[64:, :64].reshape(2, WIDTH, 64),
+        packed[48:64],
+    )
 
 
 def solution(mesh):

time: 93.8 us -> 79.7 us (0.85)
  local copies, waits for them, and re-layouts: 14.5 us -> 2.69 us
  Pallas kernels: 77.1 us -> 76 us
    unnamed x28 -> x0, local copies, waits for them, and re-layouts: 13.7 us -> none
    slice x0 -> x2, local copies, waits for them, and re-layouts: none -> 2.69 us  [the longest x1 1.4 us: body(): packed[48:64]]
    pallas_call x1, Pallas kernels: 77.1 us -> 76 us  [body(): pl.pallas_call(fused_kernel, out_shape=shape((96, LOCUS), BF16), in_specs...]
where the time goes in v3:
time: 79.7 us; the launch traced here: 79.3 us
  Pallas kernels  76 us (95%)
  local copies, waits for them, and re-layouts  2.69 us (3%)
    pallas_call x1, Pallas kernels, body(): pl.pallas_call(fused_kernel, out_shape=shape((96, LOCUS), BF16), in_specs...  76 us

profile of v3, /device:TPU:1, one launch (start us, length us, event | category | flops | bytes accessed | tf_op | source)
XLA Modules:
  0.0 79.3 jit_solution(2143419055502369070)
XLA Ops:
  0.6 76.0 %shard_map.164 = bf16[96,512]{1,0:T(8,128)(2,1)} custom-call(bf16[16,512]{1,0:T(8,128)(2,1)} %branch_hbm.1, bf16[16,512]{1,0:T(8,128)(2,1)} %gate_a_hbm.1, bf16[16,512]{1,0:T(8,128)(2,1)} %gate_b_hbm.1, bf16[16,512]{1,0:T(8,128)(2,1)} %upstream_hbm.1, bf16[16,512]{1,0:T(8,128)(2,1)} %hidden.1, f32[32,64]{1,0:T(8,128)} %bitcast.2, f32[2,16]{1,0:T(2,128)} %decay_hbm.1, ...), custom_call_target="tpu_custom_call" | custom-call | tf_op jit(solution)/shard_map/pallas_call | solution.py:555
  76.6 1.4 %fusion = (bf16[16,512]{1,0:T(8,128)(2,1)}, bf16[16,512]{1,0:T(8,128)(2,1)}, bf16[16,512]{1,0:T(8,128)(2,1)}, bf16[16,512]{1,0:T(8,128)(2,1)}) fusion(bf16[96,512]{1,0:T(8,128)(2,1)} %shard_map.164), kind=kLoop, calls=%fused_computation | loop fusion | bytes 131072 | tf_op jit(solution)/shard_map/slice | solution.py:610
  78.0 1.3 %slice.18 = bf16[32,64]{1,0:T(8,128)(2,1)} slice(bf16[96,512]{1,0:T(8,128)(2,1)} %shard_map.164), slice={[64:96], [0:64]} | slice | bytes 8192 | tf_op jit(solution)/shard_map/slice | solution.py:609

commit v4 on v3

--- a/solution.py
+++ b/solution.py
@@ -118,9 +118,11 @@
     feat,
     stage,
     msg,
+    hmsg,
     inb,
+    inh,
     sbuf,
-    gate,
+    third,
     cross,
     dcat,
     ybuf,
@@ -130,7 +132,9 @@
     rcat,
     obuf,
     outb,
+    outh,
     got,
+    goth,
     part_f,
     got_f,
     part_w,
@@ -143,14 +147,20 @@
     f_recv,
     b_send,
     b_recv,
+    h_send,
+    h_recv,
     g_send,
     g_recv,
     c_send,
     c_recv,
     s_send,
     s_recv,
+    e_send,
+    e_recv,
     o_send,
     o_recv,
+    k_send,
+    k_recv,
     p_send,
     p_recv,
     w_send,
@@ -209,8 +219,9 @@
         pltpu.make_async_copy(source, target, a_sem.at[index]).wait()
     stage_rows(0, branch[...].astype(F32))
     stage_rows(4, gate_a[...].astype(F32))
-    stage_rows(256, gate_b[...].astype(F32))
-    stage_rows(260, upstream[...].astype(F32))
+    stage_rows(8, gate_b[...].astype(F32))
+    stage_rows(12, upstream[...].astype(F32))
+    msg[...] = stage[...].astype(BF16)
     rate = decay[...]
     scale = jnp.sqrt(less_one(-2.0 * rate) / less_one(-2.0 * rate * (SEQ * LOCUS)))
     diagonal = lax.broadcasted_iota(jnp.int32, (WIDTH, WIDTH), 0) == lax.broadcasted_iota(
@@ -238,6 +249,23 @@
 
     for step in range(1, CH):
         send(hidden, feat.at[mine], f_send, f_recv, seq, lax.rem(ch + step, CH))
+
+    slot = tile_rows(seq, 16)
+
+    @pl.loop(0, WIDTH)
+    def _(step):
+        to = lax.rem(channel + step, WIDTH)
+        owner = owner_of(to, ch)
+        piece = msg.at[tile_rows(to, 16)]
+
+        @pl.when(owner != seq)
+        def _():
+            send(piece, inb.at[slot], b_send, b_recv, owner, ch)
+
+        @pl.when(owner == seq)
+        def _():
+            pltpu.make_async_copy(piece, inb.at[slot], b_recv).start()
+
     drain(feat.at[pl.ds(0, 3 * WIDTH)], f_recv)
     weight = readout[...]
     high, rest = halves(weight)
@@ -247,27 +275,25 @@
     )
     filt = (triple[:32] + triple[32:64] + triple[64:]) * windows[...]
     for order in range(2):
-        value = filt[order * WIDTH : (order + 1) * WIDTH]
-        first = value.astype(BF16).astype(F32)
-        stage_rows(order * 256 + 8, first)
-        stage_rows(order * 256 + 12, value - first)
-    msg[...] = stage[...].astype(BF16)
-    slot = tile_rows(seq, 16)
+        for part in range(4):
+            hmsg[pl.ds(order * 64 + part, WIDTH, stride=4), :] = filt[
+                order * WIDTH : (order + 1) * WIDTH, part * 128 : (part + 1) * 128
+            ]
 
     @pl.loop(0, WIDTH)
     def _(step):
         to = lax.rem(channel + step, WIDTH)
         for core in range(2):
             owner = owner_of(to, ch) + core
-            piece = msg.at[tile_rows(core * WIDTH + to, 16)]
+            piece = hmsg.at[tile_rows(core * WIDTH + to, 4)]
 
             @pl.when(owner != seq)
             def _():
-                send(piece, inb.at[slot], b_send, b_recv, owner, ch)
+                send(piece, inh.at[tile_rows(seq, 4)], h_send, h_recv, owner, ch)
 
             @pl.when(owner == seq)
             def _():
-                pltpu.make_async_copy(piece, inb.at[slot], b_recv).start()
+                pltpu.make_async_copy(piece, inh.at[tile_rows(seq, 4)], h_recv).start()
 
     def chunks(body):
         @pl.loop(0, 8)
@@ -372,39 +398,35 @@
     def _():
         for index, (source, target) in enumerate(tables):
             pltpu.make_async_copy(source, target, t_sem.at[index]).wait()
-        drain(inb, b_recv)
         first_core = role == 0
+
+        @pl.when(first_core)
+        def _():
+            drain(inb, b_recv)
+            swap(inb, inb, g_send, g_recv).start()
+
+        @pl.when(jnp.logical_not(first_core))
+        def _():
+            drain(inb, g_recv)
+
         sign = jnp.where(first_core, 1.0, -1.0).astype(F32)
         sbuf[...] = inb[...].astype(F32)
         for half in range(2):
-            second = load(1, half)
-            rows = pl.ds(half * 128, 128)
-            place(half, 0, *halves(load(0, half) * jnp.where(first_core, 1.0, second)))
-            place(half, 1, load(2, half).astype(BF16), load(3, half).astype(BF16))
-
-            @pl.when(first_core)
-            def _():
-                gate[rows, :] = second
-
-        @pl.when(first_core)
-        def _():
-            swap(gate, gate, g_send, g_recv).start()
-
+            value = jnp.where(first_core, load(0, half), load(2, half) * load(3, half))
+            place(half, 0, *halves(value))
+        drain(inh, h_recv)
+        for half in range(2):
+            value = jnp.concatenate(
+                [inh[pl.ds(2 * half + part, SEQ, stride=4), :] for part in range(2)], 1
+            )
+            place(half, 1, *halves(value))
         forward(2, 0)
         inverse(((0, 1, sign, 1.0),))
-
-        @pl.when(first_core)
-        def _():
-            drain(gate, g_send)
-
-        @pl.when(jnp.logical_not(first_core))
-        def _():
-            drain(gate, g_recv)
 
         for half in range(2):
             rows = pl.ds(half * 128, 128)
             value = block(half, 0)
-            place(half, 0, *halves(gate[rows, :] * value))
+            place(half, 0, *halves(load(1, half) * value))
 
             @pl.when(first_core)
             def _():
@@ -426,43 +448,60 @@
         copy.wait()
         inverse(((3, 1, -sign, 1.0), (3, 0, -1.0, sign)))
 
-        @pl.when(first_core)
-        def _():
-            drain(cross, c_recv)
-            for half in range(2):
-                store(0, half, block(half, 0))
-                store(1, half, load(3, half) * cross[pl.ds(half * 128, 128), :])
-
-        @pl.when(jnp.logical_not(first_core))
-        def _():
-            drain(cross, c_send)
-            for half in range(2):
-                store(0, half, block(half, 0) * load(1, half))
-
         for half in range(2):
             value = block(half, 1)
-            first = value.astype(BF16).astype(F32)
-            store(2, half, first)
-            store(3, half, value - first)
-        outb[...] = sbuf[...].astype(BF16)
-        home = tile_rows(role * WIDTH + channel, 16)
+            for part in range(2):
+                outh[pl.ds(2 * half + part, SEQ, stride=4), :] = value[
+                    :, part * 128 : (part + 1) * 128
+                ]
+        home = role * WIDTH + channel
 
         @pl.loop(1, SEQ)
         def _(step):
             to = lax.rem(seq + step, SEQ)
-            send(outb.at[tile_rows(to, 16)], got.at[home], o_send, o_recv, to, ch)
-
-        pltpu.make_async_copy(outb.at[slot], got.at[home], o_recv).start()
-
-    drain(got, o_recv)
-    stage[...] = got[...].astype(F32)
-
-    def taken(row):
-        return jnp.concatenate(
-            [stage[pl.ds(row + part, WIDTH, stride=16), :] for part in range(4)], 1
-        )
-
-    grads = jnp.concatenate([taken(8) + taken(12), taken(264) + taken(268)], 0)
+            send(outh.at[tile_rows(to, 4)], goth.at[tile_rows(home, 4)], o_send, o_recv, to, ch)
+
+        pltpu.make_async_copy(
+            outh.at[tile_rows(seq, 4)], goth.at[tile_rows(home, 4)], o_recv
+        ).start()
+
+        @pl.when(jnp.logical_not(first_core))
+        def _():
+            for half in range(2):
+                third[pl.ds(half * 128, 128), :] = block(half, 0) * load(3, half)
+            swap(third, third, e_send, e_recv).start()
+
+        @pl.when(first_core)
+        def _():
+            drain(cross, c_recv)
+            for half in range(2):
+                rows = pl.ds(half * 128, 128)
+                store(0, half, block(half, 0))
+                store(1, half, load(3, half) * cross[rows, :])
+            drain(third, e_recv)
+            for half in range(2):
+                store(2, half, third[pl.ds(half * 128, 128), :])
+            outb[...] = sbuf[...].astype(BF16)
+
+            @pl.loop(1, SEQ)
+            def _(step):
+                to = lax.rem(seq + step, SEQ)
+                send(
+                    outb.at[tile_rows(to, 16)], got.at[tile_rows(channel, 16)], k_send, k_recv, to, ch
+                )
+
+            pltpu.make_async_copy(outb.at[slot], got.at[tile_rows(channel, 16)], k_recv).start()
+
+    drain(goth, o_recv)
+    grads = jnp.concatenate(
+        [
+            jnp.concatenate(
+                [goth[pl.ds(order * 64 + part, WIDTH, stride=4), :] for part in range(4)], 1
+            )
+            for order in range(2)
+        ],
+        0,
+    )
     dhw = grads * windows[...] * (1.0 / math.sqrt(SEQ * LOCUS))
     dhi, dlo = halves(dhw)
     whi, wlo = high, middle
@@ -491,9 +530,6 @@
         send(part_f.at[tile_rows(to, WIDTH)], got_f.at[mine], p_send, p_recv, seq, to)
     got_w[tile_rows(channel, 16), :] = part_w[...]
     got_f[mine, :] = part_f[mine, :]
-    packed[pl.ds(0, WIDTH), :] = taken(0).astype(BF16)
-    packed[pl.ds(16, WIDTH), :] = taken(4).astype(BF16)
-    packed[pl.ds(32, WIDTH), :] = taken(256).astype(BF16)
     drain(got_w.at[pl.ds(0, 15 * 16)], w_recv)
     total = got_w[pl.ds(0, 16), :]
     for index in range(1, 16):
@@ -511,18 +547,37 @@
     for index in range(1, CH):
         summed = summed + got_f[pl.ds(WIDTH * index, WIDTH), :]
     packed[pl.ds(48, WIDTH), :] = summed.astype(BF16)
+    drain(got, k_recv)
+    stage[...] = got[...].astype(F32)
+    for index in range(3):
+        packed[pl.ds(16 * index, WIDTH), :] = jnp.concatenate(
+            [stage[pl.ds(4 * index + part, WIDTH, stride=16), :] for part in range(4)], 1
+        ).astype(BF16)
     drain(feat.at[pl.ds(0, 3 * WIDTH)], f_send)
     drain(got_f.at[pl.ds(0, 3 * WIDTH)], p_send)
     drain(got_w.at[pl.ds(0, 15 * 16)], w_send)
 
     @pl.when(is_owner)
     def _():
-        drain(msg.at[pl.ds(0, (2 * WIDTH - 1) * 16)], b_send)
-        drain(outb.at[pl.ds(0, (SEQ - 1) * 16)], o_send)
+        drain(hmsg.at[pl.ds(0, (2 * WIDTH - 1) * 4)], h_send)
+        drain(outh.at[pl.ds(0, (SEQ - 1) * 4)], o_send)
+
+        @pl.when(role == 0)
+        def _():
+            drain(msg.at[pl.ds(0, (WIDTH - 1) * 16)], b_send)
+            drain(inb, g_send)
+            drain(outb.at[pl.ds(0, (SEQ - 1) * 16)], k_send)
+
+        @pl.when(role == 1)
+        def _():
+            drain(msg, b_send)
+            drain(cross, c_send)
+            drain(third, e_send)
 
     @pl.when(jnp.logical_not(is_owner))
     def _():
         drain(msg, b_send)
+        drain(hmsg, h_send)
 
     drain(got_v.at[pl.ds(0, 7 * 16)], v_recv)
     total = got_v[pl.ds(0, 16), :]
@@ -564,9 +619,11 @@
             pltpu.VMEM((2, WIDTH), F32),
             pltpu.VMEM((2 * WIDTH, LOCUS), F32),
             pltpu.VMEM((64, LOCUS), BF16),
+            pltpu.VMEM((256, 128), F32),
+            pltpu.VMEM((256, 128), BF16),
+            pltpu.VMEM((128, 128), F32),
+            pltpu.VMEM((2048, 128), BF16),
             pltpu.VMEM((512, 128), F32),
-            pltpu.VMEM((512, 128), BF16),
-            pltpu.VMEM((2048, 128), BF16),
             pltpu.VMEM((2048, 128), F32),
             pltpu.VMEM((256, 256), F32),
             pltpu.VMEM((256, 256), F32),
@@ -578,7 +635,9 @@
             pltpu.VMEM((1536, 512), BF16),
             pltpu.VMEM((256, 512), F32),
             pltpu.VMEM((2048, 128), BF16),
-            pltpu.VMEM((512, 128), BF16),
+            pltpu.VMEM((512, 128), F32),
+            pltpu.VMEM((256, 128), BF16),
+            pltpu.VMEM((128, 128), F32),
             pltpu.VMEM((64, LOCUS), F32),
             pltpu.VMEM((64, LOCUS), F32),
             pltpu.VMEM((16, 128), F32),
@@ -588,7 +647,7 @@
             pltpu.SemaphoreType.DMA((6,)),
             pltpu.SemaphoreType.DMA((7,)),
         ]
-        + [dma] * 18,
+        + [dma] * 24,
         compiler_params=pltpu.CompilerParams(
             collective_id=1, has_side_effects=True, vmem_limit_bytes=VMEM_BYTES
         ),

time: 79.7 us -> 72.3 us (0.907)
  Pallas kernels: 76 us -> 68.6 us
    pallas_call x1, Pallas kernels: 76 us -> 68.6 us  [body(): pl.pallas_call(fused_kernel, out_shape=shape((96, LOCUS), BF16), in_specs...]
where the time goes in v4:
time: 72.3 us; the launch traced here: 71.9 us
  Pallas kernels  68.6 us (95%)
  local copies, waits for them, and re-layouts  2.69 us (4%)
    pallas_call x1, Pallas kernels, body(): pl.pallas_call(fused_kernel, out_shape=shape((96, LOCUS), BF16), in_specs...  68.6 us

profile of v4, /device:TPU:1, one launch (start us, length us, event | category | flops | bytes accessed | tf_op | source)
XLA Modules:
  0.0 71.9 jit_solution(18206522004316192915)
XLA Ops:
  0.6 68.6 %shard_map.164 = bf16[96,512]{1,0:T(8,128)(2,1)} custom-call(bf16[16,512]{1,0:T(8,128)(2,1)} %branch_hbm.1, bf16[16,512]{1,0:T(8,128)(2,1)} %gate_a_hbm.1, bf16[16,512]{1,0:T(8,128)(2,1)} %gate_b_hbm.1, bf16[16,512]{1,0:T(8,128)(2,1)} %upstream_hbm.1, bf16[16,512]{1,0:T(8,128)(2,1)} %hidden.1, f32[32,64]{1,0:T(8,128)} %bitcast.2, f32[2,16]{1,0:T(2,128)} %decay_hbm.1, ...), custom_call_target="tpu_custom_call" | custom-call | tf_op jit(solution)/shard_map/pallas_call | solution.py:610
  69.2 1.4 %fusion = (bf16[16,512]{1,0:T(8,128)(2,1)}, bf16[16,512]{1,0:T(8,128)(2,1)}, bf16[16,512]{1,0:T(8,128)(2,1)}, bf16[16,512]{1,0:T(8,128)(2,1)}) fusion(bf16[96,512]{1,0:T(8,128)(2,1)} %shard_map.164), kind=kLoop, calls=%fused_computation | loop fusion | bytes 131072 | tf_op jit(solution)/shard_map/slice | solution.py:669
  70.6 1.3 %slice.18 = bf16[32,64]{1,0:T(8,128)(2,1)} slice(bf16[96,512]{1,0:T(8,128)(2,1)} %shard_map.164), slice={[64:96], [0:64]} | slice | bytes 8192 | tf_op jit(solution)/shard_map/slice | solution.py:668

commit v5 on v4

--- a/solution.py
+++ b/solution.py
@@ -178,6 +178,21 @@
     barrier = pltpu.get_barrier_semaphore()
     mine = tile_rows(ch, WIDTH)
 
+    def everyone(visit):
+        for ahead in (2, 1, 3, 0):
+            high = lax.rem(lax.div(low, 2) + ahead, 4)
+
+            @pl.loop(0, 32)
+            def _(step):
+                to = lax.rem(channel + lax.div(step, 2), 16) * 8 + high * 2 + lax.rem(step, 2)
+                if ahead:
+                    visit(to)
+                else:
+
+                    @pl.when(to != seq)
+                    def _():
+                        visit(to)
+
     for step in range(1, CH):
         greet(barrier, seq, lax.rem(ch + step, CH))
 
@@ -309,11 +324,10 @@
         zcat[place, pl.ds(base + 512, 256)] = low
         zcat[place, pl.ds(base + 1024, 256)] = high
 
-    def forward(count, slot):
+    def forward(count, slot, start=0, after_half=None):
         width = 256 * count
-        ybuf[:, pl.ds(0, width)] = jnp.dot(
-            w1[...], dcat[:, pl.ds(0, width)], preferred_element_type=F32
-        )
+        taken = pl.ds(256 * start, width)
+        ybuf[:, pl.ds(0, width)] = jnp.dot(w1[...], dcat[:, taken], preferred_element_type=F32)
         for index in range(count):
             columns = pl.ds(index * 256, 256)
 
@@ -325,11 +339,18 @@
                 put_rows(place, 256, re * ci + im * cr)
 
             chunks(body)
-        spec[pl.ds(slot * 256, width), :] = jnp.dot(
-            zcat[pl.ds(0, width), :], w2[...], preferred_element_type=F32
-        )
-
-    def inverse(pairs):
+        if after_half is None:
+            spec[pl.ds(slot * 256, width), :] = jnp.dot(
+                zcat[pl.ds(0, width), :], w2[...], preferred_element_type=F32
+            )
+        else:
+            for half in range(2):
+                spec[pl.ds(slot * 256 + 128 * half, 128), :] = jnp.dot(
+                    zcat[pl.ds(128 * half, 128), :], w2[...], preferred_element_type=F32
+                )
+                after_half(half)
+
+    def inverse(pairs, start=0):
         count = len(pairs)
         width = 256 * count
         for index, (left, right, sign, flip) in enumerate(pairs):
@@ -360,7 +381,7 @@
                     rcat[after(base + 1024, step), columns] = high
 
             chunks(body)
-        obuf[:, pl.ds(0, width)] = jnp.dot(
+        obuf[:, pl.ds(256 * start, width)] = jnp.dot(
             w1t[...], rcat[:, pl.ds(0, width)], preferred_element_type=F32
         )
 
@@ -414,13 +435,14 @@
         for half in range(2):
             value = jnp.where(first_core, load(0, half), load(2, half) * load(3, half))
             place(half, 0, *halves(value))
+        forward(1, 0)
         drain(inh, h_recv)
         for half in range(2):
             value = jnp.concatenate(
                 [inh[pl.ds(2 * half + part, SEQ, stride=4), :] for part in range(2)], 1
             )
             place(half, 1, *halves(value))
-        forward(2, 0)
+        forward(1, 1, 1)
         inverse(((0, 1, sign, 1.0),))
 
         for half in range(2):
@@ -436,17 +458,21 @@
             def _():
                 cross[rows, :] = value
 
+        def hand_over(half, start=True):
+            rows, theirs = pl.ds(512 + 128 * half, 128), pl.ds(768 + 128 * half, 128)
+            copy = swap(spec.at[rows], spec.at[theirs], s_send.at[half], s_recv.at[half])
+            if start:
+                copy.start()
+            return copy
+
         @pl.when(jnp.logical_not(first_core))
         def _():
             swap(cross, cross, c_send, c_recv).start()
 
-        forward(1, 2)
-        mine = pl.ds(512, 256)
-        theirs = pl.ds(768, 256)
-        copy = swap(spec.at[mine], spec.at[theirs], s_send, s_recv)
-        copy.start()
-        copy.wait()
-        inverse(((3, 1, -sign, 1.0), (3, 0, -1.0, sign)))
+        forward(1, 2, 0, hand_over)
+        for half in range(2):
+            hand_over(half, False).wait()
+        inverse(((3, 0, -1.0, sign),), 1)
 
         for half in range(2):
             value = block(half, 1)
@@ -464,6 +490,7 @@
         pltpu.make_async_copy(
             outh.at[tile_rows(seq, 4)], goth.at[tile_rows(home, 4)], o_recv
         ).start()
+        inverse(((3, 1, -sign, 1.0),))
 
         @pl.when(jnp.logical_not(first_core))
         def _():
@@ -504,6 +531,20 @@
     )
     dhw = grads * windows[...] * (1.0 / math.sqrt(SEQ * LOCUS))
     dhi, dlo = halves(dhw)
+    double = lax.dot_general(
+        jnp.concatenate([dhi, dlo], 0),
+        feat[...],
+        (((1,), (1,)), ((), ())),
+        preferred_element_type=F32,
+    )
+    total = double[:32] + double[32:]
+    part_w[...] = jnp.concatenate([total[:WIDTH], total[WIDTH:]], 1)
+
+    @pl.loop(1, 16)
+    def _(step):
+        to = lax.rem(channel + step, 16) * 8 + low
+        send(part_w, got_w.at[tile_rows(channel, 16)], w_send, w_recv, to, ch)
+
     whi, wlo = high, middle
     part_f[...] = lax.dot_general(
         jnp.concatenate([whi, whi, wlo], 0),
@@ -511,20 +552,6 @@
         (((0,), (0,)), ((), ())),
         preferred_element_type=F32,
     )
-    double = lax.dot_general(
-        jnp.concatenate([dhi, dlo], 0),
-        feat[...],
-        (((1,), (1,)), ((), ())),
-        preferred_element_type=F32,
-    )
-    total = double[:32] + double[32:]
-    part_w[...] = jnp.concatenate([total[:WIDTH], total[WIDTH:]], 1)
-
-    @pl.loop(1, 16)
-    def _(step):
-        to = lax.rem(channel + step, 16) * 8 + low
-        send(part_w, got_w.at[tile_rows(channel, 16)], w_send, w_recv, to, ch)
-
     for step in range(1, CH):
         to = lax.rem(ch + step, CH)
         send(part_f.at[tile_rows(to, WIDTH)], got_f.at[mine], p_send, p_recv, seq, to)
@@ -647,7 +674,9 @@
             pltpu.SemaphoreType.DMA((6,)),
             pltpu.SemaphoreType.DMA((7,)),
         ]
-        + [dma] * 24,
+        + [dma] * 10
+        + [pltpu.SemaphoreType.DMA((2,))] * 2
+        + [dma] * 12,
         compiler_params=pltpu.CompilerParams(
             collective_id=1, has_side_effects=True, vmem_limit_bytes=VMEM_BYTES
         ),

time: 72.3 us -> 70.3 us (0.972)
  Pallas kernels: 68.6 us -> 66.6 us
    pallas_call x1, Pallas kernels: 68.6 us -> 66.6 us  [body(): pl.pallas_call(fused_kernel, out_shape=shape((96, LOCUS), BF16), in_specs...]
where the time goes in v5:
time: 70.3 us; the launch traced here: 69.9 us
  Pallas kernels  66.6 us (95%)
  local copies, waits for them, and re-layouts  2.69 us (4%)
    pallas_call x1, Pallas kernels, body(): pl.pallas_call(fused_kernel, out_shape=shape((96, LOCUS), BF16), in_specs...  66.6 us

profile of v5, /device:TPU:1, one launch (start us, length us, event | category | flops | bytes accessed | tf_op | source)
XLA Modules:
  0.0 69.9 jit_solution(4141619241559413625)
XLA Ops:
  0.6 66.6 %shard_map.164 = bf16[96,512]{1,0:T(8,128)(2,1)} custom-call(bf16[16,512]{1,0:T(8,128)(2,1)} %branch_hbm.1, bf16[16,512]{1,0:T(8,128)(2,1)} %gate_a_hbm.1, bf16[16,512]{1,0:T(8,128)(2,1)} %gate_b_hbm.1, bf16[16,512]{1,0:T(8,128)(2,1)} %upstream_hbm.1, bf16[16,512]{1,0:T(8,128)(2,1)} %hidden.1, f32[32,64]{1,0:T(8,128)} %bitcast.2, f32[2,16]{1,0:T(2,128)} %decay_hbm.1, ...), custom_call_target="tpu_custom_call" | custom-call | tf_op jit(solution)/shard_map/pallas_call | solution.py:637
  67.3 1.4 %fusion = (bf16[16,512]{1,0:T(8,128)(2,1)}, bf16[16,512]{1,0:T(8,128)(2,1)}, bf16[16,512]{1,0:T(8,128)(2,1)}, bf16[16,512]{1,0:T(8,128)(2,1)}) fusion(bf16[96,512]{1,0:T(8,128)(2,1)} %shard_map.164), kind=kLoop, calls=%fused_computation | loop fusion | bytes 131072 | tf_op jit(solution)/shard_map/slice | solution.py:698
  68.7 1.3 %slice.18 = bf16[32,64]{1,0:T(8,128)(2,1)} slice(bf16[96,512]{1,0:T(8,128)(2,1)} %shard_map.164), slice={[64:96], [0:64]} | slice | bytes 8192 | tf_op jit(solution)/shard_map/slice | solution.py:697

commit v6 on v5

--- a/solution.py
+++ b/solution.py
@@ -20,7 +20,7 @@
 
 
 def owner_of(channel, group):
-    high = lax.rem(lax.div(channel, 4) + lax.rem(channel, 4) + 3 * group, 4)
+    high = lax.rem(lax.div(channel, 4) + lax.rem(channel, 4) + group, 4)
     return channel * 8 + 2 * high
 
 
@@ -102,6 +102,7 @@
     twr_hbm,
     twi_hbm,
     packed,
+    sums,
     w1,
     w1t,
     w2,
@@ -173,25 +174,11 @@
     channel = lax.div(seq, 8)
     low = lax.rem(seq, 8)
     role = lax.rem(seq, 2)
-    is_owner = owner_of(channel, ch) == seq - role
+    over = lax.rem(ch + 2, CH)
+    is_owner = owner_of(channel, over) == seq - role
     partner = seq + 1 - 2 * role
     barrier = pltpu.get_barrier_semaphore()
     mine = tile_rows(ch, WIDTH)
-
-    def everyone(visit):
-        for ahead in (2, 1, 3, 0):
-            high = lax.rem(lax.div(low, 2) + ahead, 4)
-
-            @pl.loop(0, 32)
-            def _(step):
-                to = lax.rem(channel + lax.div(step, 2), 16) * 8 + high * 2 + lax.rem(step, 2)
-                if ahead:
-                    visit(to)
-                else:
-
-                    @pl.when(to != seq)
-                    def _():
-                        visit(to)
 
     for step in range(1, CH):
         greet(barrier, seq, lax.rem(ch + step, CH))
@@ -219,9 +206,9 @@
 
     @pl.when(is_owner)
     def _():
-        @pl.loop(1, SEQ)
+        @pl.loop(0, SEQ)
         def _(step):
-            greet(barrier, lax.rem(seq + step, SEQ), ch)
+            greet(barrier, lax.rem(seq + step, SEQ), over)
 
         for index, (source, target) in enumerate(tables):
             pltpu.make_async_copy(source, target, t_sem.at[index]).start()
@@ -254,13 +241,7 @@
             -column(rate, order) * position
         ) * column(scale, order)
 
-    @pl.when(is_owner)
-    def _():
-        pl.semaphore_wait(barrier, 2 * WIDTH - 1 + CH - 1)
-
-    @pl.when(jnp.logical_not(is_owner))
-    def _():
-        pl.semaphore_wait(barrier, 2 * WIDTH + CH - 1)
+    pl.semaphore_wait(barrier, 2 * WIDTH + CH - 1)
 
     for step in range(1, CH):
         send(hidden, feat.at[mine], f_send, f_recv, seq, lax.rem(ch + step, CH))
@@ -270,16 +251,8 @@
     @pl.loop(0, WIDTH)
     def _(step):
         to = lax.rem(channel + step, WIDTH)
-        owner = owner_of(to, ch)
         piece = msg.at[tile_rows(to, 16)]
-
-        @pl.when(owner != seq)
-        def _():
-            send(piece, inb.at[slot], b_send, b_recv, owner, ch)
-
-        @pl.when(owner == seq)
-        def _():
-            pltpu.make_async_copy(piece, inb.at[slot], b_recv).start()
+        send(piece, inb.at[slot], b_send, b_recv, owner_of(to, ch), over)
 
     drain(feat.at[pl.ds(0, 3 * WIDTH)], f_recv)
     weight = readout[...]
@@ -299,16 +272,9 @@
     def _(step):
         to = lax.rem(channel + step, WIDTH)
         for core in range(2):
+            piece = hmsg.at[tile_rows(core * WIDTH + to, 4)]
             owner = owner_of(to, ch) + core
-            piece = hmsg.at[tile_rows(core * WIDTH + to, 4)]
-
-            @pl.when(owner != seq)
-            def _():
-                send(piece, inh.at[tile_rows(seq, 4)], h_send, h_recv, owner, ch)
-
-            @pl.when(owner == seq)
-            def _():
-                pltpu.make_async_copy(piece, inh.at[tile_rows(seq, 4)], h_recv).start()
+            send(piece, inh.at[tile_rows(seq, 4)], h_send, h_recv, owner, over)
 
     def chunks(body):
         @pl.loop(0, 8)
@@ -482,14 +448,11 @@
                 ]
         home = role * WIDTH + channel
 
-        @pl.loop(1, SEQ)
+        @pl.loop(0, SEQ)
         def _(step):
             to = lax.rem(seq + step, SEQ)
-            send(outh.at[tile_rows(to, 4)], goth.at[tile_rows(home, 4)], o_send, o_recv, to, ch)
-
-        pltpu.make_async_copy(
-            outh.at[tile_rows(seq, 4)], goth.at[tile_rows(home, 4)], o_recv
-        ).start()
+            send(outh.at[tile_rows(to, 4)], goth.at[tile_rows(home, 4)], o_send, o_recv, to, over)
+
         inverse(((3, 1, -sign, 1.0),))
 
         @pl.when(jnp.logical_not(first_core))
@@ -510,14 +473,12 @@
                 store(2, half, third[pl.ds(half * 128, 128), :])
             outb[...] = sbuf[...].astype(BF16)
 
-            @pl.loop(1, SEQ)
+            target = got.at[tile_rows(channel, 16)]
+
+            @pl.loop(0, SEQ)
             def _(step):
                 to = lax.rem(seq + step, SEQ)
-                send(
-                    outb.at[tile_rows(to, 16)], got.at[tile_rows(channel, 16)], k_send, k_recv, to, ch
-                )
-
-            pltpu.make_async_copy(outb.at[slot], got.at[tile_rows(channel, 16)], k_recv).start()
+                send(outb.at[tile_rows(to, 16)], target, k_send, k_recv, to, over)
 
     drain(goth, o_recv)
     grads = jnp.concatenate(
@@ -586,31 +547,25 @@
 
     @pl.when(is_owner)
     def _():
-        drain(hmsg.at[pl.ds(0, (2 * WIDTH - 1) * 4)], h_send)
-        drain(outh.at[pl.ds(0, (SEQ - 1) * 4)], o_send)
+        drain(outh, o_send)
 
         @pl.when(role == 0)
         def _():
-            drain(msg.at[pl.ds(0, (WIDTH - 1) * 16)], b_send)
             drain(inb, g_send)
-            drain(outb.at[pl.ds(0, (SEQ - 1) * 16)], k_send)
+            drain(outb, k_send)
 
         @pl.when(role == 1)
         def _():
-            drain(msg, b_send)
             drain(cross, c_send)
             drain(third, e_send)
 
-    @pl.when(jnp.logical_not(is_owner))
-    def _():
-        drain(msg, b_send)
-        drain(hmsg, h_send)
-
+    drain(msg, b_send)
+    drain(hmsg, h_send)
     drain(got_v.at[pl.ds(0, 7 * 16)], v_recv)
     total = got_v[pl.ds(0, 16), :]
     for index in range(1, 8):
         total = total + got_v[pl.ds(16 * index, 16), :]
-    packed[pl.ds(64, 2 * WIDTH), pl.ds(0, 64)] = jnp.concatenate([total[:, :64], total[:, 64:]], 0).astype(BF16)
+    sums[...] = jnp.concatenate([total[:, :64], total[:, 64:]], 0).astype(BF16)
     drain(got_v.at[pl.ds(0, 7 * 16)], v_send)
 
 
@@ -634,11 +589,11 @@
     dma = pltpu.SemaphoreType.DMA
     readout = kernel_readout_matrix.reshape(2 * WIDTH, CH * WIDTH)
     tables = [jnp.asarray(table) for table in make_tables()]
-    packed = pl.pallas_call(
+    packed, sums = pl.pallas_call(
         fused_kernel,
-        out_shape=shape((96, LOCUS), BF16),
+        out_shape=(shape((64, LOCUS), BF16), shape((2 * WIDTH, 64), BF16)),
         in_specs=[pl.BlockSpec(memory_space=pltpu.HBM)] * 13,
-        out_specs=vmem(1)[0],
+        out_specs=tuple(vmem(2)),
         scratch_shapes=[pltpu.VMEM(table.shape, table.dtype) for table in tables]
         + [pltpu.VMEM((WIDTH, LOCUS), BF16)] * 4
         + [
@@ -694,7 +649,7 @@
         packed[:16],
         packed[16:32],
         packed[32:48],
-        packed[64:, :64].reshape(2, WIDTH, 64),
+        sums.reshape(2, WIDTH, 64),
         packed[48:64],
     )
 

time: 70.3 us -> 68.9 us (0.980)
  Pallas kernels: 66.6 us -> 64.8 us
    pallas_call x1, Pallas kernels: 66.6 us -> 64.8 us  [body(): pl.pallas_call(fused_kernel, out_shape=(shape((64, LOCUS), BF16), shape((...]
    unnamed x0 -> x1, local copies, waits for them, and re-layouts: none -> 1.29 us
    slice x1 -> x0, local copies, waits for them, and re-layouts: 1.29 us -> none  [body(): packed[64:, :64].reshape(2, WIDTH, 64)]
where the time goes in v6:
time: 68.9 us; the launch traced here: 68.1 us
  Pallas kernels  64.8 us (94%)
  local copies, waits for them, and re-layouts  2.69 us (4%)
    pallas_call x1, Pallas kernels, body(): pl.pallas_call(fused_kernel, out_shape=(shape((64, LOCUS), BF16), shape((...  64.8 us
    slice x1, local copies, waits for them, and re-layouts, body(): packed[48:64]  1.4 us

profile of v6, /device:TPU:1, one launch (start us, length us, event | category | flops | bytes accessed | tf_op | source)
XLA Modules:
  0.0 68.1 jit_solution(16441897317847114019)
XLA Ops:
  0.6 64.8 %shard_map.164 = (bf16[64,512]{1,0:T(8,128)(2,1)}, bf16[32,64]{1,0:T(8,128)(2,1)}) custom-call(bf16[16,512]{1,0:T(8,128)(2,1)} %branch_hbm.1, bf16[16,512]{1,0:T(8,128)(2,1)} %gate_a_hbm.1, bf16[16,512]{1,0:T(8,128)(2,1)} %gate_b_hbm.1, bf16[16,512]{1,0:T(8,128)(2,1)} %upstream_hbm.1, bf16[16,512]{1,0:T(8,128)(2,1)} %hidden.1, f32[32,64]{1,0:T(8,128)} %bitcast.2, ...), custom_call_target="tpu_custom_call" | custom-call | tf_op jit(solution)/shard_map/pallas_call | solution.py:592
  65.4 1.4 %fusion = (bf16[16,512]{1,0:T(8,128)(2,1)}, bf16[16,512]{1,0:T(8,128)(2,1)}, bf16[16,512]{1,0:T(8,128)(2,1)}, bf16[16,512]{1,0:T(8,128)(2,1)}) fusion(bf16[64,512]{1,0:T(8,128)(2,1)} %get-tuple-element.7), kind=kLoop, calls=%fused_computation | loop fusion | bytes 131072 | tf_op jit(solution)/shard_map/slice | solution.py:653
  66.8 1.3 %copy.19 = bf16[2,16,64]{2,1,0:T(8,128)(2,1)} copy(bf16[2,16,64]{2,1,0:T(8,128)(2,1)} %bitcast.3) | data formatting | bytes 8192
